TPU v7x, 512 devices: a whole 4x4x16 slice. The times are simulated.
512 devices in a mesh: row: 32 (over y, z_lo), col: 16 (over z_hi, x, core).
Axes of the slice: x: 4, y: 4, z: 16 (z_hi: 2, z_lo: 8; z = z_hi * 8 + z_lo), core: 2. Of those that a mesh axis runs over, the one named last changes fastest.
Arguments:
- picture_vectors: bfloat16 [20480, 1152], P(('row', 'col')), may hold values from -8 to 8
- caption_vectors: bfloat16 [20480, 1152], P(('col', 'row')), may hold values from -8 to 8
- scale_exponent: float32 [1], replicated, may hold values from 4 to 4.7
- score_shift: float32 [1], replicated, may hold values from -15 to -11
Outputs:
- image_grad: float32 [20480, 1152], P(('row', 'col'))
- text_grad: float32 [20480, 1152], P(('col', 'row'))
All inputs are finite; a program needn't handle non-finite values.
Results may differ from a plain program's by a relative error of at most 0.029.
Values may be sent and summed in bfloat16 or wider, within the bound.
A program may use at most 64 MiB of HBM per device.

v0:
```python
import jax
import jax.numpy as jnp
from jax import lax
from jax.sharding import PartitionSpec as P


def unit_rows(values):
    values = values.astype(jnp.float32)
    inverse = lax.rsqrt(jnp.sum(values * values, axis=1, keepdims=True) + 1e-06)
    return (values * inverse, inverse)


def pairwise_weight(
    image_batch, text_batch, image_indices, text_indices, smoothing_multiplier, block_offset
):
    inner_products = lax.dot_general(
        image_batch, text_batch, (((1,), (1,)), ((), ())), preferred_element_type=jnp.float32
    )
    pair_logits = smoothing_multiplier * inner_products + block_offset
    label_signs = jnp.where(image_indices[:, None] == text_indices[None, :], 1.0, -1.0).astype(
        jnp.float32
    )
    return (
        -label_signs * smoothing_multiplier * jax.nn.sigmoid(-label_signs * pair_logits)
    ).astype(jnp.bfloat16)


def body(picture_vectors, caption_vectors, scale_exponent, score_shift):
    shard_rows = picture_vectors.shape[0]
    entry_number = lax.axis_size("row")
    col_count = lax.axis_size("col")
    row_index = lax.axis_index("row")
    column_position = lax.axis_index("col")
    smoothing_multiplier = jnp.exp(scale_exponent[0])
    block_offset = score_shift[0]
    image_unit, image_inverse = unit_rows(picture_vectors)
    text_unit, text_inverse = unit_rows(caption_vectors)
    image_half = image_unit.astype(jnp.bfloat16)
    text_halfway = text_unit.astype(jnp.bfloat16)
    image_block_rows = lax.all_gather(image_half, "col", axis=0, tiled=True)
    block_rows = col_count * shard_rows
    group_rows = entry_number * shard_rows
    image_indices = row_index * block_rows + jnp.arange(block_rows, dtype=jnp.int32)
    text_base = column_position * group_rows
    text_block_rows = lax.all_gather(text_halfway, "row", axis=0, tiled=True)
    text_indices = text_base + jnp.arange(group_rows, dtype=jnp.int32)
    weight_values = pairwise_weight(
        image_block_rows,
        text_block_rows,
        image_indices,
        text_indices,
        smoothing_multiplier,
        block_offset,
    )
    image_part = jnp.dot(weight_values, text_block_rows, preferred_element_type=jnp.float32)
    image_dir = lax.psum_scatter(
        image_part.astype(jnp.bfloat16), "col", scatter_dimension=0, tiled=True
    ).astype(jnp.float32)
    text_part = lax.dot_general(
        weight_values,
        image_block_rows,
        (((0,), (0,)), ((), ())),
        preferred_element_type=jnp.float32,
    )
    text_dir = lax.psum_scatter(
        text_part.astype(jnp.bfloat16), "row", scatter_dimension=0, tiled=True
    ).astype(jnp.float32)
    image_grad = (
        image_dir - image_unit * jnp.sum(image_unit * image_dir, axis=1, keepdims=True)
    ) * image_inverse
    text_grad = (
        text_dir - text_unit * jnp.sum(text_unit * text_dir, axis=1, keepdims=True)
    ) * text_inverse
    return (image_grad, text_grad)


def solution(mesh):
    return jax.shard_map(
        body,
        mesh=mesh,
        in_specs=(P(("row", "col"), None), P(("col", "row"), None), P(), P()),
        out_specs=(P(("row", "col"), None), P(("col", "row"), None)),
        check_vma=False,
    )
```

profile of v0, /device:TPU:2, one launch (start us, length us, event | category | flops | bytes accessed | tf_op | source)
XLA Modules:
  0.0 700.0 jit_solution(3994280587103864333)
XLA Ops:
  7.2 0.0 all-gather.3.cloned.1.call-start
  7.2 1.0 fusion.12
  8.2 1.6 fusion.11
  9.9 0.0 all-gather.3.cloned.1.call-update
  9.9 0.0 all-gather.5.cloned.1.call-start
  9.9 1.0 fusion.13
  11.0 1.6 fusion.9
  12.6 0.0 all-gather.5.cloned.1.call-update
  12.6 0.0 reduce-scatter.8.cloned.1.call-start
  14.0 85.7 %all-gather.3.cloned.1.call-done = bf16[640,1152]{1,0:T(8,128)(2,1)} async-done(((bf16[40,1152]{1,0:T(8,128)(2,1)}), bf16[640,1152]{1,0:T(8,128)(2,1)}) %all-gather.3.cloned.1.call-update) | async-done | bytes 1474576 | tf_op jit(solution)/shard_map/all_gather | solution.py:40
  99.7 225.1 %all-gather.5.cloned.1.call-done = bf16[1280,1152]{1,0:T(8,128)(2,1)} async-done(((bf16[40,1152]{1,0:T(8,128)(2,1)}), bf16[1280,1152]{1,0:T(8,128)(2,1)}) %all-gather.5.cloned.1.call-update) | async-done | bytes 2949136 | tf_op jit(solution)/shard_map/all_gather | solution.py:45
  324.8 0.0 copy-start.2
  324.8 5.5 fusion.7
  330.3 0.0 copy-done.2
  330.3 0.0 copy-start.3
  330.3 3.4 convolution_convert_fusion.1
  333.8 0.0 reduce-scatter.8.cloned.1.call-update
  333.8 0.0 reduce-scatter.10.cloned.1.call-start
  333.8 0.0 copy-done.3
  333.8 4.0 convolution_convert_fusion
  337.9 0.0 copy-start
  337.9 0.0 copy-start.1
  337.9 0.0 reduce-scatter.10.cloned.1.call-update
  337.9 107.3 %reduce-scatter.8.cloned.1.call-done = bf16[40,1152]{1,0:T(8,128)(2,1)} async-done(((bf16[640,1152]{1,0:T(8,128)(2,1)}), bf16[40,1152]{1,0:T(8,128)(2,1)}) %reduce-scatter.8.cloned.1.call-update) | async-done | bytes 92176
  445.2 0.0 copy-done
  445.2 1.1 fusion.14
  446.3 1.7 fusion.15
  448.0 242.7 %reduce-scatter.10.cloned.1.call-done = bf16[40,1152]{1,0:T(8,128)(2,1)} async-done(((bf16[1280,1152]{1,0:T(8,128)(2,1)}), bf16[40,1152]{1,0:T(8,128)(2,1)}) %reduce-scatter.10.cloned.1.call-update) | async-done | bytes 92176
  690.7 0.0 copy-done.1
  690.7 1.1 fusion.16
  691.8 1.7 fusion.17
  (4 shorter events, 0.0 us)
Async XLA Ops:
  7.2 92.6 %all-gather.3.cloned.1.call-start = ((), (), s32[]{:S(2)}) async-start(), calls=%async_computation.2 | async-start | bytes 1566720 | tf_op jit(solution)/shard_map/all_gather | solution.py:40
  9.9 314.9 %all-gather.5.cloned.1.call-start = ((), (), s32[]{:S(2)}) async-start(), calls=%async_computation.3 | async-start | bytes 3041280 | tf_op jit(solution)/shard_map/all_gather | solution.py:45
  12.6 432.6 %reduce-scatter.8.cloned.1.call-start = ((), (), s32[]{:S(2)}) async-start(), calls=%async_computation.4 | async-start | bytes 1566720
  324.8 5.5 copy-start.2
  330.3 3.5 copy-start.3
  333.8 356.9 %reduce-scatter.10.cloned.1.call-start = ((), (), s32[]{:S(2)}) async-start(), calls=%async_computation.5 | async-start | bytes 3041280
  337.9 107.4 %copy-start = (bf16[40,1152]{1,0:T(8,128)(2,1)S(1)}, bf16[40,1152]{1,0:T(8,128)(2,1)}, u32[]{:S(2)}) copy-start(bf16[40,1152]{1,0:T(8,128)(2,1)} %param.4) | copy-start | bytes 276484
  337.9 352.9 %copy-start.1 = (bf16[40,1152]{1,0:T(8,128)(2,1)S(1)}, bf16[40,1152]{1,0:T(8,128)(2,1)}, u32[]{:S(2)}) copy-start(bf16[40,1152]{1,0:T(8,128)(2,1)} %param.5) | copy-start | bytes 276484
Sparse Core Ops, SparseCore 0:
  11.9 87.7 all-gather.2
  102.4 222.3 all-gather.4
  333.9 111.2 reduce-scatter.7
  447.9 242.7 reduce-scatter.9
where the time goes:
time: 700 us
  waiting for transfers between devices  661 us (94%)
  between operations  15.2 us (2%)
  matrix products  12.9 us (2%)
  other arithmetic  10.8 us (2%)
    unnamed x6, waiting for transfers between devices  350 us
    all_gather x1, waiting for transfers between devices, body(): text_block_rows = lax.all_gather(text_halfway, 'row', axis=0, tiled=True)  225 us
    all_gather x1, waiting for transfers between devices, body(): image_block_rows = lax.all_gather(image_half, 'col', axis=0, tiled=True)  85.7 us
  transfers between devices with their start and end apart: 4, of which 4 were waited for; matrix products, arithmetic and copies ran while one was open for 1% of the time, Pallas kernels for 0%

commit v1 on v0

v1 whole, which is shorter than its diff:
```python
import functools

import jax
import jax.numpy as jnp
from jax import lax
from jax.experimental import pallas as pl
from jax.experimental.pallas import tpu as pltpu
from jax.sharding import PartitionSpec as P

MESH = pl.DeviceIdType.MESH
D = 1152
SHARD = 40
UNIT = 80
CHUNK = 384
NCHUNK = 3
SLOTS = [
    (0, 0), (1, 0), (-1, 0), (2, 0), (0, 1), (0, -1), (1, 1), (1, -1),
    (-1, 1), (-1, -1), (2, 1), (2, -1), (0, 2), (1, 2), (-1, 2), (2, 2),
]
SLOT = {ab: i for i, ab in enumerate(SLOTS)}
RIGHT = (0, 2)
LEFT = (1, -1)
N_IMG = 16 * UNIT
N_TXT = 8 * UNIT
LINE = (0, 1, -1, 2)


def unit_rows(values):
    values = values.astype(jnp.float32)
    inverse = lax.rsqrt(jnp.sum(values * values, axis=1, keepdims=True) + 1e-06)
    return values * inverse, inverse


def cols(j):
    return pl.ds(j * CHUNK, CHUNK)


def kernel(
    pic, cap, scale, shift, gi, gt,
    rpic, rcap, oimg, img, txt, wt, pbuf, qbuf,
    psend, pd, rsb, rr, tf, tfr,
    rel_in, fin_in, half_in, afin_in, bsend, asend, last_send, last_in, sib_send, sib_in,
    ssem, rsem,
):
    r = lax.axis_index("row")
    q = lax.axis_index("col")
    x, y, z, c = (q % 8) // 2, r // 8, (q // 8) * 8 + r % 8, q % 2

    def dev(x, y, z, c):
        x, y, z = (x + 4) % 4, (y + 4) % 4, (z + 16) % 16
        return (y * 8 + z % 8, (z // 8) * 8 + x * 2 + c)

    sib = dev(x, y, z, 1 - c)
    sg = 1 - 2 * c

    def along_a(s):
        return dev(x + s * (1 - c), y + s * c, z, c)

    def along_b(s):
        return dev(x + s * c, y + s * (1 - c), z, c)

    ahead = dev(x, y, z + 2 * sg, c)
    behind = dev(x, y, z - 2 * sg, c)
    is0 = c == 0
    is1 = c == 1

    ids = {}
    started = []

    def rcopy(key, src, dst, to):
        i = ids.setdefault(key, len(ids))
        return pltpu.make_async_remote_copy(
            src_ref=src, dst_ref=dst, send_sem=ssem.at[i], recv_sem=rsem.at[i],
            device_id=to, device_id_type=MESH,
        )

    def send(key, src, dst, to, when=None):
        cp = rcopy(key, src, dst, to)
        if when is None:
            cp.start()
        else:
            pl.when(when)(cp.start)
        started.append((cp, when))

    def recv(key, dst, when=None):
        cp = rcopy(key, dst, dst, sib)
        if when is None:
            cp.wait_recv()
        else:
            pl.when(when)(cp.wait_recv)

    barrier = pltpu.get_barrier_semaphore()

    def greet(to):
        pl.semaphore_signal(barrier, inc=1, device_id=to, device_id_type=MESH)

    for to in (sib, along_a(1), along_a(-1), along_b(1), along_b(-1), ahead, behind, dev(x, y, z + 1, 1)):
        greet(to)

    @pl.when(is1)
    def _():
        greet(dev(x, y, z - 1, 1))
        greet(dev(x, y, z - 1, 0))
        pl.semaphore_wait(barrier, 10)

    @pl.when(is0)
    def _():
        pl.semaphore_wait(barrier, 8)

    send("rcap", cap, rcap, sib)
    send("rpic", pic, rpic, sib)
    own_txt = unit_rows(cap[...])[0]
    own_img = unit_rows(pic[...])[0]

    def both(mine, other):
        return jnp.concatenate(
            [jnp.where(is0, mine, other), jnp.where(is0, other, mine)], axis=0
        ).astype(jnp.bfloat16)

    recv("rcap", rcap)
    txt[0:UNIT] = both(own_txt, unit_rows(rcap[...])[0])

    def t_rows(slot):
        return pl.ds(pl.multiple_of(slot * UNIT, UNIT), UNIT)

    def fslot(k):
        return 2 * k - 1 + c

    def gslot(k):
        return 2 * k - c

    for j in range(NCHUNK):
        send(("t", 1, j), txt.at[0:UNIT, cols(j)], txt.at[t_rows(fslot(1)), cols(j)], ahead)
    recv("rpic", rpic)
    unit_img = both(own_img, unit_rows(rpic[...])[0])
    oimg[...] = unit_img

    def i_rows(slot):
        return pl.ds(slot * UNIT, UNIT)

    @pl.when(is0)
    def _():
        img[0:UNIT] = unit_img

    send("shift", oimg, img.at[0:UNIT], dev(x, y, z + 1, 1), when=is1)

    def isend(slot, to_slot, to):
        send(("i", to_slot), img.at[i_rows(slot)], img.at[i_rows(to_slot)], to)

    def irecv(slot):
        recv(("i", slot), img.at[i_rows(slot)])

    recv("shift", img.at[0:UNIT], when=is1)
    isend(0, SLOT[-1, 0], along_a(1))
    isend(0, SLOT[1, 0], along_a(-1))
    isend(0, SLOT[0, -1], along_b(1))
    isend(0, SLOT[0, 1], along_b(-1))

    D8 = pl.ds(7 * UNIT, UNIT)

    def d8_when(j):
        return is0 if j == 0 else is1

    def text_step(k):
        rows = t_rows(fslot(k))
        for j in range(NCHUNK):
            here = txt.at[rows, cols(j)]
            recv(("t", k, j), here)
            if k < 3:
                send(("t", k + 1, j), here, txt.at[t_rows(fslot(k + 1)), cols(j)], ahead)
            else:
                send(("t8", j), here, txt.at[D8, cols(j)], ahead, when=d8_when(j))
            send(("g", k, j), here, here, sib)

    def text_d8():
        for j in range(NCHUNK):
            here = txt.at[D8, cols(j)]
            recv(("t8", j), here, when=d8_when(j))
            send(("g8", j), here, here, sib, when=d8_when(j))

    def text_got(k):
        for j in range(NCHUNK):
            recv(("g", k, j), txt.at[t_rows(gslot(k)), cols(j)])

    def text_got8():
        for j in range(NCHUNK):
            recv(("g8", j), txt.at[D8, cols(j)], when=d8_when((j == 0) * 1))

    def line_step(a):
        slot = SLOT[a, 0]
        if a == 2:
            recv(("i3", 0), img.at[pl.ds(slot * UNIT, 48)])
            recv(("i3", 1), img.at[pl.ds(slot * UNIT + 48, 32)])
        else:
            irecv(slot)
        if a == -1:
            send(("i3", 0), img.at[pl.ds(slot * UNIT, 48)], img.at[pl.ds(3 * UNIT, 48)], along_a(1))
        if a == 1:
            send(("i3", 1), img.at[pl.ds(slot * UNIT + 48, 32)], img.at[pl.ds(3 * UNIT + 48, 32)], along_a(-1))
        isend(slot, SLOT[a, -1], along_b(1))
        isend(slot, SLOT[a, 1], along_b(-1))

    def side_step(a):
        irecv(SLOT[a, -1])
        if a in RIGHT:
            isend(SLOT[a, -1], SLOT[a, 2], along_b(1))
        irecv(SLOT[a, 1])
        if a in LEFT:
            isend(SLOT[a, 1], SLOT[a, 2], along_b(-1))

    lane = lax.broadcasted_iota(jnp.int32, (1, N_IMG), 1)
    zi = (z - c + 16) % 16
    img_ids = lane
    before = None
    for s, (a, b) in enumerate(SLOTS):
        xs = (x + a * (1 - c) + b * c + 4) % 4
        ys = (y + a * c + b * (1 - c) + 4) % 4
        base = ((ys * 8 + zi % 8) * 16 + (zi // 8) * 8 + xs * 2) * SHARD
        if s == 0:
            img_ids = img_ids + base
        else:
            img_ids = img_ids + jnp.where(lane >= s * UNIT, base - before - UNIT, 0)
        before = base

    row_in = lax.broadcasted_iota(jnp.int32, (UNIT, 1), 0)
    row_in = row_in + jnp.where(row_in >= SHARD, 32 * SHARD - SHARD, 0)

    def txt_ids(slot):
        step = 0 if slot == 0 else (8 if slot == 7 else (-2 * ((slot + 1) // 2) if slot % 2 else slot))
        zt = (z + step + 16) % 16
        return row_in + (((zt // 8) * 8 + x * 2) * 32 + y * 8 + zt % 8) * SHARD

    smooth = jnp.exp(jnp.full((1, 128), scale[0], jnp.float32))[:, :1]
    offset = shift[0]

    def weights(t0, t1, i0, i1):
        dots = lax.dot_general(
            txt[t0:t1], img[i0:i1], (((1,), (1,)), ((), ())), preferred_element_type=jnp.float32
        )
        logits = smooth * dots + offset
        tid = jnp.concatenate([txt_ids(s) for s in range(t0 // UNIT, t1 // UNIT)], axis=0)
        match = tid == img_ids[:, i0:i1]
        value = smooth / (1.0 + jnp.exp(jnp.where(match, logits, -logits)))
        wt[t0:t1, i0:i1] = jnp.where(match, -value, value).astype(jnp.bfloat16)

    line_step(-1)
    line_step(1)
    text_step(1)
    side_step(0)
    line_step(2)
    text_got(1)
    text_step(2)
    side_step(1)
    weights(0, 240, 0, 640)
    side_step(-1)
    text_got(2)
    weights(240, 400, 0, 640)
    text_step(3)
    side_step(2)
    irecv(SLOT[0, 2])
    irecv(SLOT[1, 2])
    irecv(SLOT[-1, 2])
    text_d8()
    irecv(SLOT[2, 2])
    weights(0, 240, 640, 1280)
    weights(240, 400, 640, 1280)
    text_got(3)
    text_got8()
    weights(400, 640, 0, 640)
    weights(400, 640, 640, 1280)

    def text_part(t0, t1):
        pbuf[t0:t1] = jnp.dot(wt[t0:t1], img[...], preferred_element_type=jnp.float32)

    def image_part(i0, i1):
        qbuf[i0:i1] = lax.dot_general(
            wt[:, i0:i1], txt[...], (((0,), (0,)), ((), ())), preferred_element_type=jnp.float32
        )

    def part_out(k):
        psend[k] = pbuf[t_rows(gslot(k))].astype(jnp.bfloat16)
        for j in range(NCHUNK):
            send(("p", k, j), psend.at[k, :, cols(j)], pd.at[k, :, cols(j)], sib)

    def part_out8():
        psend[0] = pbuf[D8].astype(jnp.bfloat16)
        for j in range(NCHUNK):
            send(("p", 0, j), psend.at[0, :, cols(j)], pd.at[0, :, cols(j)], sib, when=d8_when((j == 0) * 1))

    def back8():
        for j in range(NCHUNK):
            @pl.when(d8_when(j))
            def _(j=j):
                recv(("p", 0, j), pd.at[0, :, cols(j)])
                total = pbuf[D8, cols(j)] + pd[0, :, cols(j)].astype(jnp.float32)
                rsb[0, :, cols(j)] = total.astype(jnp.bfloat16)
            send(("b", 0, j), rsb.at[0, :, cols(j)], rr.at[3, :, cols(j)], behind, when=d8_when(j))

    def back_chunk(k, j):
        recv(("p", k, j), pd.at[k, :, cols(j)])
        total = pbuf[t_rows(fslot(k)), cols(j)] + pd[k, :, cols(j)].astype(jnp.float32)
        if k < 3:
            recv(("b", k + 1, j), rr.at[k, :, cols(j)])
            rsb[k, :, cols(j)] = (total + rr[k, :, cols(j)].astype(jnp.float32)).astype(jnp.bfloat16)
        else:
            mine = d8_when(j)

            @pl.when(mine)
            def _():
                recv(("b", 0, j), rr.at[3, :, cols(j)])
                rsb[k, :, cols(j)] = (total + rr[3, :, cols(j)].astype(jnp.float32)).astype(jnp.bfloat16)

            @pl.when(jnp.logical_not(mine))
            def _():
                rsb[k, :, cols(j)] = total.astype(jnp.bfloat16)
        send(("b", k, j), rsb.at[k, :, cols(j)], rr.at[k - 1, :, cols(j)], behind)

    def back(k):
        for j in range(NCHUNK):
            back_chunk(k, j)

    def q_unit(slot):
        return qbuf[slot * UNIT:(slot + 1) * UNIT]

    def opposite(n):
        a = LINE[n]
        bsend[n] = q_unit(SLOT[a, 2]).astype(jnp.bfloat16)
        send(("ro", a), bsend.at[n], rel_in.at[n], along_b(1 if a in RIGHT else -1))

    def toward(n, s):
        a = LINE[n]
        m = 4 + n if s == 1 else 8 + n
        total = q_unit(SLOT[a, s])
        if (a in RIGHT) == (s == 1):
            recv(("ro", a), rel_in.at[n])
            total = total + rel_in[n].astype(jnp.float32)
        bsend[m] = total.astype(jnp.bfloat16)
        send(("rf", a, s), bsend.at[m], fin_in.at[m - 4], along_b(s))

    def line_total(n):
        a = LINE[n]
        recv(("rf", a, 1), fin_in.at[n])
        recv(("rf", a, -1), fin_in.at[4 + n])
        return (
            q_unit(SLOT[a, 0]) + fin_in[n].astype(jnp.float32) + fin_in[4 + n].astype(jnp.float32)
        )

    text_part(400, 640)
    part_out8()
    part_out(3)
    image_part(896, 1280)
    for n in range(4):
        opposite(n)
    back8()
    for j in range(NCHUNK):
        @pl.when(jnp.logical_not(d8_when(j)))
        def _(j=j):
            recv(("p", 3, j), pd.at[3, :, cols(j)])
            total = pbuf[t_rows(fslot(3)), cols(j)] + pd[3, :, cols(j)].astype(jnp.float32)
            rsb[3, :, cols(j)] = total.astype(jnp.bfloat16)
        send(("b", 3, j), rsb.at[3, :, cols(j)], rr.at[2, :, cols(j)], behind, when=jnp.logical_not(d8_when(j)))
    image_part(256, 896)
    for n in range(4):
        for s in (1, -1):
            if (LINE[n] in RIGHT) != (s == 1):
                toward(n, s)
    for j in range(NCHUNK):
        @pl.when(d8_when(j))
        def _(j=j):
            recv(("p", 3, j), pd.at[3, :, cols(j)])
            recv(("b", 0, j), rr.at[3, :, cols(j)])
            total = pbuf[t_rows(fslot(3)), cols(j)] + pd[3, :, cols(j)].astype(jnp.float32)
            rsb[3, :, cols(j)] = (total + rr[3, :, cols(j)].astype(jnp.float32)).astype(jnp.bfloat16)
        send(("b", 3, j), rsb.at[3, :, cols(j)], rr.at[2, :, cols(j)], behind, when=d8_when(j))
    text_part(240, 400)
    part_out(2)
    for n in range(4):
        for s in (1, -1):
            if (LINE[n] in RIGHT) == (s == 1):
                toward(n, s)
    text_part(0, 240)
    part_out(1)
    back(2)
    image_part(0, 256)
    opp = line_total(3)
    asend[0] = opp.astype(jnp.bfloat16)
    send(("ra", 0), asend.at[0, pl.ds(0, 48)], half_in.at[pl.ds(0, 48)], along_a(1))
    send(("ra", 1), asend.at[0, pl.ds(48, 32)], half_in.at[pl.ds(48, 32)], along_a(-1))
    back(1)
    plus = line_total(1)
    recv(("ra", 0), half_in.at[pl.ds(0, 48)])
    asend[1] = jnp.concatenate(
        [plus[:48] + half_in[0:48].astype(jnp.float32), plus[48:]], axis=0
    ).astype(jnp.bfloat16)
    send(("rb", 0), asend.at[1], afin_in.at[0], along_a(1))
    minus = line_total(2)
    recv(("ra", 1), half_in.at[pl.ds(48, 32)])
    asend[2] = jnp.concatenate(
        [minus[:48], minus[48:] + half_in[48:80].astype(jnp.float32)], axis=0
    ).astype(jnp.bfloat16)
    send(("rb", 1), asend.at[2], afin_in.at[1], along_a(-1))

    for j in range(NCHUNK):
        recv(("b", 1, j), rr.at[0, :, cols(j)])
    tf[...] = pbuf[0:UNIT] + rr[0].astype(jnp.float32)

    def half(core):
        return pl.ds(pl.multiple_of(core * SHARD, SHARD), SHARD)

    send("tf", tf.at[half(1 - c)], tfr, sib)

    own = line_total(0)
    recv(("rb", 0), afin_in.at[0])
    recv(("rb", 1), afin_in.at[1])
    own = own + afin_in[0].astype(jnp.float32) + afin_in[1].astype(jnp.float32)

    @pl.when(is1)
    def _():
        for h in range(2):
            last_send[h, 0:SHARD] = own[h * SHARD:(h + 1) * SHARD].astype(jnp.bfloat16)
            last_send[h, SHARD:48] = jnp.zeros((48 - SHARD, D), jnp.bfloat16)

    @pl.when(is0)
    def _():
        sib_send[...] = own

    send(("last", 0), last_send.at[0], last_in, dev(x, y, z - 1, 0), when=is1)
    send(("last", 1), last_send.at[1], last_in, dev(x, y, z - 1, 1), when=is1)
    send("sib", sib_send.at[pl.ds(SHARD, SHARD)], sib_in, sib, when=is0)

    recv("tf", tfr)
    v, v_inv = unit_rows(cap[...])
    text_dir = tf[half(c)] + tfr[...]
    gt[...] = (text_dir - v * jnp.sum(v * text_dir, axis=1, keepdims=True)) * v_inv

    recv("sib", sib_in, when=is1)
    recv(("last", 0), last_in, when=is0)
    recv(("last", 1), last_in, when=is1)

    @pl.when(is0)
    def _():
        sib_in[...] = sib_send[0:SHARD]

    u, u_inv = unit_rows(pic[...])
    image_dir = sib_in[...] + last_in[0:SHARD].astype(jnp.float32)
    gi[...] = (image_dir - u * jnp.sum(u * image_dir, axis=1, keepdims=True)) * u_inv

    for cp, when in started:
        if when is None:
            cp.wait_send()
        else:
            pl.when(when)(cp.wait_send)


def body(picture_vectors, caption_vectors, scale_exponent, score_shift):
    bf16, f32 = jnp.bfloat16, jnp.float32
    vmem = pl.BlockSpec(memory_space=pltpu.VMEM)
    smem = pl.BlockSpec(memory_space=pltpu.SMEM)
    out = jax.ShapeDtypeStruct((SHARD, D), f32)
    return pl.pallas_call(
        kernel,
        out_shape=(out, out),
        in_specs=[vmem, vmem, smem, smem],
        out_specs=(vmem, vmem),
        scratch_shapes=[
            pltpu.VMEM((SHARD, D), bf16),
            pltpu.VMEM((SHARD, D), bf16),
            pltpu.VMEM((UNIT, D), bf16),
            pltpu.VMEM((N_IMG, D), bf16),
            pltpu.VMEM((N_TXT, D), bf16),
            pltpu.VMEM((N_TXT, N_IMG), bf16),
            pltpu.VMEM((N_TXT, D), f32),
            pltpu.VMEM((N_IMG, D), f32),
            pltpu.VMEM((4, UNIT, D), bf16),
            pltpu.VMEM((4, UNIT, D), bf16),
            pltpu.VMEM((4, UNIT, D), bf16),
            pltpu.VMEM((4, UNIT, D), bf16),
            pltpu.VMEM((UNIT, D), f32),
            pltpu.VMEM((SHARD, D), f32),
            pltpu.VMEM((4, UNIT, D), bf16),
            pltpu.VMEM((8, UNIT, D), bf16),
            pltpu.VMEM((UNIT, D), bf16),
            pltpu.VMEM((2, UNIT, D), bf16),
            pltpu.VMEM((12, UNIT, D), bf16),
            pltpu.VMEM((3, UNIT, D), bf16),
            pltpu.VMEM((2, 48, D), bf16),
            pltpu.VMEM((48, D), bf16),
            pltpu.VMEM((UNIT, D), f32),
            pltpu.VMEM((SHARD, D), f32),
            pltpu.SemaphoreType.DMA((128,)),
            pltpu.SemaphoreType.DMA((128,)),
        ],
        compiler_params=pltpu.CompilerParams(
            collective_id=0, has_side_effects=True, vmem_limit_bytes=56 * 2**20
        ),
    )(picture_vectors, caption_vectors, scale_exponent, score_shift)


def solution(mesh):
    return jax.shard_map(
        body,
        mesh=mesh,
        in_specs=(P(("row", "col"), None), P(("col", "row"), None), P(), P()),
        out_specs=(P(("row", "col"), None), P(("col", "row"), None)),
        check_vma=False,
    )
```

time: 700 us -> 82.8 us (0.12)
  the two profiles are of different devices: /device:TPU:2 before, /device:TPU:1 now
where the time goes in v1:
time: 82.8 us; the launch traced here: 82.5 us
  Pallas kernels  78.2 us (94%)
  local copies, waits for them, and re-layouts  2.32 us (3%)
  between operations  1.94 us (2%)
    pallas_call x1, Pallas kernels, body(): pl.pallas_call(kernel, out_shape=(out, out), in_specs=[vmem, vmem, smem,...  78.2 us
    unnamed x4, local copies, waits for them, and re-layouts  2.32 us

profile of v1, /device:TPU:1, one launch (start us, length us, event | category | flops | bytes accessed | tf_op | source)
XLA Modules:
  0.0 82.5 jit_solution(3215615891670063835)
XLA Ops:
  1.9 78.2 %shard_map.59 = (f32[40,1152]{1,0:T(8,128)}, f32[40,1152]{1,0:T(8,128)}) custom-call(bf16[40,1152]{1,0:T(8,128)(2,1)} %pic.1, bf16[40,1152]{1,0:T(8,128)(2,1)} %cap.1, f32[1]{0:T(128)S(6)} %copy.8.scale, f32[1]{0:T(128)S(6)} %copy.9.shift), custom_call_target="tpu_custom_call" | custom-call | tf_op jit(solution)/shard_map/pallas_call | solution.py:460
  80.1 0.0 copy-start
  80.2 1.6 %copy.10 = f32[40,1152]{1,0:T(8,128)} copy(f32[40,1152]{1,0:T(8,128)} %get-tuple-element.4) | data formatting | bytes 368640
  81.8 0.0 copy-done
  81.8 0.7 copy.11
Async XLA Ops:
  80.1 1.7 %copy-start = (f32[40,1152]{1,0:T(8,128)S(1)}, f32[40,1152]{1,0:T(8,128)}, u32[]{:S(2)}) copy-start(f32[40,1152]{1,0:T(8,128)} %get-tuple-element.5) | copy-start | bytes 552964

commit v2 on v0

v2 whole, which is shorter than its diff:
```python
import jax
import jax.numpy as jnp
from jax import lax
from jax.experimental import pallas as pl
from jax.experimental.pallas import tpu as pltpu
from jax.sharding import PartitionSpec as P

MESH = pl.DeviceIdType.MESH
D = 1152
SHARD = 40
UNIT = 80
SLOTS = (
    (0, 0), (1, 0), (-1, 0), (2, 0), (0, 1), (0, -1), (1, 1), (1, -1),
    (-1, 1), (-1, -1), (2, 1), (2, -1), (0, 2), (1, 2), (-1, 2), (2, 2),
)
SLOT = {ab: i for i, ab in enumerate(SLOTS)}
RIGHT = (0, 2)
LINE = (0, 1, -1, 2)
N_IMG = 16 * UNIT
N_TXT = 8 * UNIT
T_ROWS = ((0, 32), (32, 32), (64, 16))
I_ROWS = ((0, 48), (48, 32))
FAR = ((0,), (1, 2))
T_GROUPS = ((0, 240), (240, 400), (400, 560), (560, 640))
I_GROUPS = ((0, 640), (640, 1024), (1024, 1280))
Q_GROUPS = ((896, 1280), (256, 896), (0, 256))
ORDER = (
    (
        ('t', 0, 0), ('t', 0, 1), ('t', 0, 2), ('i', 0, 0), ('i', 0, 1), ('i', 1, 0), ('i', 2, 0), ('i', 4, 0),
        ('i', 5, 0), ('t', 1, 0), ('i', 1, 1), ('i', 2, 1), ('i', 4, 1), ('i', 5, 1), ('t', 1, 1), ('t', 1, 2),
        ('i', 3, 1), ('t', 2, 0), ('i', 3, 0), ('i', 6, 0), ('i', 7, 0), ('i', 8, 0), ('i', 9, 0), ('t', 2, 1),
        ('i', 6, 1), ('t', 2, 2), ('i', 12, 0), ('i', 8, 1), ('i', 7, 1), ('W', 0, 0), ('t', 3, 0), ('i', 9, 1),
        ('W', 1, 0), ('i', 10, 1), ('i', 12, 1), ('t', 3, 1), ('i', 10, 0), ('t', 3, 2), ('i', 11, 1), ('i', 13, 0),
        ('W', 2, 0), ('i', 11, 0), ('i', 14, 0), ('t', 4, 0), ('W', 0, 1), ('W', 1, 1), ('i', 13, 1), ('W', 2, 1),
        ('i', 14, 1), ('i', 15, 1), ('W', 3, 0), ('W', 3, 1), ('i', 15, 0), ('W', 0, 2), ('W', 1, 2), ('W', 2, 2),
        ('W', 3, 2), ('P', 2), ('pp', 3), ('P', 3), ('pp', 0), ('Q', 0), ('ro', 0, 0), ('ro', 0, 1), ('ro', 1, 0),
        ('ro', 1, 1), ('ro', -1, 0), ('ro', -1, 1), ('ro', 2, 0), ('ro', 2, 1), ('Q', 1), ('rf', 0, -1, 0),
        ('rf', 0, -1, 1), ('rf', 1, 1, 0), ('rf', 1, 1, 1), ('rf', -1, 1, 0), ('rf', -1, 1, 1), ('rf', 2, -1, 0),
        ('rf', 2, -1, 1), ('b', 3, 1), ('b', 3, 2), ('b', 0, 0), ('rf', 0, 1, 0), ('rf', 1, -1, 0), ('rf', 0, 1, 1),
        ('P', 1), ('pp', 2), ('rf', 1, -1, 1), ('rf', 2, 1, 0), ('rf', -1, -1, 0), ('Q', 2), ('rf', 2, 1, 1),
        ('rf', -1, -1, 1), ('P', 0), ('pp', 1), ('b', 2, 1), ('b', 2, 2), ('b', 3, 0), ('b', 1, 1), ('la', 1, 1),
        ('b', 1, 2), ('la', 2, 0), ('la', -1, 0), ('la', 2, 1), ('b', 2, 0), ('la', 1, 0), ('la', -1, 1),
        ('b', 1, 0), ('own',), ('tf',), ('gt',), ('gi',),
    ),
    (
        ('t', 0, 0), ('t', 0, 1), ('t', 0, 2), ('i', 0, 0), ('i', 0, 1), ('t', 1, 0), ('t', 1, 1), ('t', 1, 2),
        ('i', 1, 0), ('i', 2, 0), ('i', 4, 0), ('i', 5, 0), ('i', 1, 1), ('i', 2, 1), ('i', 4, 1), ('i', 5, 1),
        ('t', 2, 0), ('t', 2, 1), ('t', 2, 2), ('i', 6, 0), ('i', 7, 0), ('i', 8, 0), ('i', 9, 0), ('t', 3, 0),
        ('i', 3, 1), ('i', 6, 1), ('i', 12, 0), ('i', 8, 1), ('i', 7, 1), ('t', 3, 1), ('i', 9, 1), ('i', 13, 0),
        ('t', 3, 2), ('i', 3, 0), ('W', 0, 0), ('i', 12, 1), ('i', 14, 0), ('W', 1, 0), ('i', 11, 1), ('i', 10, 1),
        ('W', 2, 0), ('i', 13, 1), ('t', 4, 1), ('i', 14, 1), ('i', 11, 0), ('t', 4, 2), ('W', 3, 0), ('Q', 2),
        ('i', 10, 0), ('i', 15, 1), ('W', 0, 1), ('W', 1, 1), ('W', 2, 1), ('W', 3, 1), ('Q', 1), ('i', 15, 0),
        ('rf', 0, -1, 0), ('rf', 0, -1, 1), ('rf', 1, 1, 0), ('rf', 1, 1, 1), ('rf', -1, 1, 0), ('rf', -1, 1, 1),
        ('W', 0, 2), ('W', 1, 2), ('W', 2, 2), ('W', 3, 2), ('P', 2), ('pp', 3), ('b', 3, 0), ('P', 3), ('pp', 0),
        ('b', 0, 1), ('b', 0, 2), ('Q', 0), ('ro', 0, 0), ('ro', 0, 1), ('ro', 1, 0), ('ro', 1, 1), ('ro', -1, 0),
        ('ro', -1, 1), ('ro', 2, 0), ('rf', 2, -1, 0), ('ro', 2, 1), ('rf', 2, -1, 1), ('P', 1), ('pp', 2), ('P', 0),
        ('pp', 1), ('b', 2, 0), ('rf', 0, 1, 0), ('b', 3, 1), ('rf', 1, -1, 0), ('rf', 0, 1, 1), ('b', 3, 2),
        ('rf', 1, -1, 1), ('rf', 2, 1, 0), ('rf', -1, -1, 0), ('rf', 2, 1, 1), ('rf', -1, -1, 1), ('b', 1, 0),
        ('b', 2, 1), ('la', 2, 0), ('b', 2, 2), ('la', 2, 1), ('la', 1, 1), ('la', -1, 0), ('la', 1, 0), ('b', 1, 1),
        ('la', -1, 1), ('b', 1, 2), ('own',), ('tf',), ('gt',), ('gi',),
    ),
)


def unit_rows(values):
    values = values.astype(jnp.float32)
    inverse = lax.rsqrt(jnp.sum(values * values, axis=1, keepdims=True) + 1e-06)
    return values * inverse, inverse


def kernel(
    pic, cap, scale, shift, gi, gt,
    raw_cap, raw_a, raw_b, img, txt, wt, pbuf, qbuf,
    psend, pd, rsb, rr, tf, tfr,
    rel_in, fin_in, half_in, afin_in, bsend, asend, last_send, last_in, sib_send, sib_in,
    ssem, rsem,
):
    r = lax.axis_index("row")
    q = lax.axis_index("col")
    x, y, z, core = (q % 8) // 2, r // 8, (q // 8) * 8 + r % 8, q % 2

    def dev(x, y, z, c):
        x, y, z = (x + 4) % 4, (y + 4) % 4, (z + 16) % 16
        return (y * 8 + z % 8, (z // 8) * 8 + x * 2 + c)

    barrier = pltpu.get_barrier_semaphore()

    def greet(to):
        pl.semaphore_signal(barrier, inc=1, device_id=to, device_id_type=MESH)

    for to in (
        dev(x, y, z, 1 - core), dev(x + 1, y, z, core), dev(x - 1, y, z, core), dev(x, y + 1, z, core),
        dev(x, y - 1, z, core), dev(x, y, z + 2, core), dev(x, y, z - 2, core), dev(x, y, z + 1, 1),
    ):
        greet(to)

    @pl.when(core == 1)
    def _():
        greet(dev(x, y, z - 1, 1))
        greet(dev(x, y, z - 1, 0))

    ids = {}
    offset = shift[0]

    def one_core(c):
        sib = dev(x, y, z, 1 - c)
        sg = 1 - 2 * c
        ahead = dev(x, y, z + 2 * sg, c)
        behind = dev(x, y, z - 2 * sg, c)
        started = []

        def along_a(s):
            return dev(x + s * (1 - c), y + s * c, z, c)

        def along_b(s):
            return dev(x + s * c, y + s * (1 - c), z, c)

        def rcopy(key, src, dst, to):
            i = ids.setdefault(key, len(ids))
            return pltpu.make_async_remote_copy(
                src_ref=src, dst_ref=dst, send_sem=ssem.at[i], recv_sem=rsem.at[i],
                device_id=to, device_id_type=MESH,
            )

        def send(key, src, dst, to):
            cp = rcopy(key, src, dst, to)
            cp.start()
            started.append(cp)

        def recv(key, dst):
            rcopy(key, dst, dst, sib).wait_recv()

        smooth = jnp.exp(jnp.full((1, 128), scale[0], jnp.float32))[:, :1]
        lane = lax.broadcasted_iota(jnp.int32, (1, N_IMG), 1)
        zi = (z - c + 16) % 16
        img_ids = lane
        before = None
        for s, (a, b) in enumerate(SLOTS):
            xs = (x + a * (1 - c) + b * c + 4) % 4
            ys = (y + a * c + b * (1 - c) + 4) % 4
            base = ((ys * 8 + zi % 8) * 16 + (zi // 8) * 8 + xs * 2) * SHARD
            if s == 0:
                img_ids = img_ids + base
            else:
                img_ids = img_ids + jnp.where(lane >= s * UNIT, base - before - UNIT, 0)
            before = base
        row_in = lax.broadcasted_iota(jnp.int32, (UNIT, 1), 0)
        row_in = row_in + jnp.where(row_in >= SHARD, 32 * SHARD - SHARD, 0)

        def txt_ids(slot):
            step = 0 if slot == 0 else (8 if slot == 7 else (-2 * ((slot + 1) // 2) if slot % 2 else slot))
            zt = (z + step + 16) % 16
            return row_in + (((zt // 8) * 8 + x * 2) * 32 + y * 8 + zt % 8) * SHARD

        own_txt = unit_rows(cap[...])[0]
        if c == 0:
            own_img = unit_rows(pic[...])[0]
        pl.semaphore_wait(barrier, 10 if c else 8)
        send("cap", cap, raw_cap, sib)
        if c == 0:
            send("pic_a", pic, raw_a, dev(x, y, z + 1, 1))
        else:
            send("pic_0", pic, raw_a, sib)
            send("pic_b", pic, raw_b, dev(x, y, z + 1, 1))

        def both(one, two):
            return jnp.concatenate([one, two], axis=0).astype(jnp.bfloat16)

        def f_slot(k):
            return 0 if k == 0 else (7 if k == 4 else 2 * k - 1 + c)

        def g_slot(k):
            return 7 if k == 4 else 2 * k - c

        def t_piece(slot, h):
            return pl.ds(slot * UNIT + T_ROWS[h][0], T_ROWS[h][1])

        def i_piece(slot, h):
            return pl.ds(slot * UNIT + I_ROWS[h][0], I_ROWS[h][1])

        got = set()

        def need(key, dst):
            if key not in got:
                got.add(key)
                recv(key, dst)

        def step_t(k, h):
            if k == 0:
                if h == 0:
                    recv("cap", raw_cap)
                    other = unit_rows(raw_cap[...])[0]
                    txt[0:UNIT] = both(own_txt, other) if c == 0 else both(other, own_txt)
            else:
                need(("t", k, h), txt.at[t_piece(f_slot(k), h)])
            here = txt.at[t_piece(f_slot(k), h)]
            if k < 3 or (k == 3 and h in FAR[c]):
                send(("t", k + 1, h), here, txt.at[t_piece(f_slot(k + 1), h)], ahead)
            if k > 0:
                send(("g", k, h), here, here, sib)

        def step_i(s, h):
            a, b = SLOTS[s]

            def forward(to_slot, to):
                send(("i", to_slot, h), img.at[i_piece(s, h)], img.at[i_piece(to_slot, h)], to)

            if s == 0:
                if h == 0:
                    if c == 0:
                        recv("pic_0", raw_a)
                        img[0:UNIT] = both(own_img, unit_rows(raw_a[...])[0])
                    else:
                        recv("pic_a", raw_a)
                        recv("pic_b", raw_b)
                        img[0:UNIT] = both(unit_rows(raw_a[...])[0], unit_rows(raw_b[...])[0])
                forward(SLOT[-1, 0], along_a(1))
                forward(SLOT[1, 0], along_a(-1))
            else:
                need(("i", s, h), img.at[i_piece(s, h)])
            if b == 0:
                if a == -1 and h == 0:
                    forward(SLOT[2, 0], along_a(1))
                if a == 1 and h == 1:
                    forward(SLOT[2, 0], along_a(-1))
                forward(SLOT[a, -1], along_b(1))
                forward(SLOT[a, 1], along_b(-1))
            if b == -1 and a in RIGHT:
                forward(SLOT[a, 2], along_b(1))
            if b == 1 and a not in RIGHT:
                forward(SLOT[a, 2], along_b(-1))

        def text_needs(slot):
            if slot == 0:
                return
            k = 4 if slot == 7 else (slot + 1) // 2
            for h in range(len(T_ROWS)):
                mine = h in FAR[c] if k == 4 else (slot % 2 == 1) == (c == 0)
                if not mine:
                    need(("g", k, h), txt.at[t_piece(slot, h)])

        def step_w(gt_, gi_):
            t0, t1 = T_GROUPS[gt_]
            i0, i1 = I_GROUPS[gi_]
            for s in range(t0 // UNIT, t1 // UNIT):
                text_needs(s)
            dots = lax.dot_general(
                txt[t0:t1], img[i0:i1], (((1,), (1,)), ((), ())), preferred_element_type=jnp.float32
            )
            logits = smooth * dots + offset
            tid = jnp.concatenate([txt_ids(s) for s in range(t0 // UNIT, t1 // UNIT)], axis=0)
            match = tid == img_ids[:, i0:i1]
            value = smooth / (1.0 + jnp.exp(jnp.where(match, logits, -logits)))
            wt[t0:t1, i0:i1] = jnp.where(match, -value, value).astype(jnp.bfloat16)

        def step_p(g):
            t0, t1 = T_GROUPS[g]
            pbuf[t0:t1] = jnp.dot(wt[t0:t1], img[...], preferred_element_type=jnp.float32)

        def step_q(g):
            i0, i1 = Q_GROUPS[g]
            qbuf[i0:i1] = lax.dot_general(
                wt[:, i0:i1], txt[...], (((0,), (0,)), ((), ())), preferred_element_type=jnp.float32
            )

        def step_pp(k):
            slot = g_slot(k) if k else 7
            psend[k] = pbuf[slot * UNIT:(slot + 1) * UNIT].astype(jnp.bfloat16)
            for h, (o, n) in enumerate(T_ROWS):
                if k > 0 or h in FAR[1 - c]:
                    send(("p", k, h), psend.at[k, pl.ds(o, n)], pd.at[k, pl.ds(o, n)], sib)

        def step_b(k, h):
            o, n = T_ROWS[h]
            slot = f_slot(k) if k else 7
            recv(("p", k, h), pd.at[k, pl.ds(o, n)])
            total = pbuf[slot * UNIT + o:slot * UNIT + o + n] + pd[k, o:o + n].astype(jnp.float32)
            more = {3: 0, 2: 3, 1: 2}.get(k)
            if k in (1, 2) or (k == 3 and h in FAR[c]):
                recv(("b", more, h), rr.at[k, pl.ds(o, n)])
                total = total + rr[k, o:o + n].astype(jnp.float32)
            rsb[k, o:o + n] = total.astype(jnp.bfloat16)
            to = 3 if k == 0 else k - 1
            send(("b", k, h), rsb.at[k, pl.ds(o, n)], rr.at[to, pl.ds(o, n)], behind)

        def step_tf():
            for h, (o, n) in enumerate(T_ROWS):
                recv(("b", 1, h), rr.at[0, pl.ds(o, n)])
            tf[...] = pbuf[0:UNIT] + rr[0].astype(jnp.float32)
            send("tf", tf.at[pl.ds((1 - c) * SHARD, SHARD)], tfr, sib)

        def step_gt():
            recv("tf", tfr)
            v, v_inv = unit_rows(cap[...])
            text_dir = tf[c * SHARD:(c + 1) * SHARD] + tfr[...]
            gt[...] = (text_dir - v * jnp.sum(v * text_dir, axis=1, keepdims=True)) * v_inv

        def q_piece(slot, h):
            o, n = I_ROWS[h]
            return qbuf[slot * UNIT + o:slot * UNIT + o + n]

        def step_ro(a, h):
            n = LINE.index(a)
            o, m = I_ROWS[h]
            bsend[n, o:o + m] = q_piece(SLOT[a, 2], h).astype(jnp.bfloat16)
            here = pl.ds(o, m)
            send(("ro", a, h), bsend.at[n, here], rel_in.at[n, here], along_b(1 if a in RIGHT else -1))

        def step_rf(a, s, h):
            n = LINE.index(a)
            o, m = I_ROWS[h]
            here = pl.ds(o, m)
            total = q_piece(SLOT[a, s], h)
            if (a in RIGHT) == (s == 1):
                recv(("ro", a, h), rel_in.at[n, here])
                total = total + rel_in[n, o:o + m].astype(jnp.float32)
            to = n if s == 1 else 4 + n
            bsend[4 + to, o:o + m] = total.astype(jnp.bfloat16)
            send(("rf", a, s, h), bsend.at[4 + to, here], fin_in.at[to, here], along_b(s))

        def line_total(a, h):
            n = LINE.index(a)
            o, m = I_ROWS[h]
            here = pl.ds(o, m)
            recv(("rf", a, 1, h), fin_in.at[n, here])
            recv(("rf", a, -1, h), fin_in.at[4 + n, here])
            return (
                q_piece(SLOT[a, 0], h)
                + fin_in[n, o:o + m].astype(jnp.float32)
                + fin_in[4 + n, o:o + m].astype(jnp.float32)
            )

        def step_la(a, h):
            o, m = I_ROWS[h]
            here = pl.ds(o, m)
            total = line_total(a, h)
            i = {2: 0, 1: 1, -1: 2}[a]
            if (a, h) in ((1, 0), (-1, 1)):
                recv(("ra", h), half_in.at[here])
                total = total + half_in[o:o + m].astype(jnp.float32)
            asend[i, o:o + m] = total.astype(jnp.bfloat16)
            if a == 2:
                send(("ra", h), asend.at[i, here], half_in.at[here], along_a(1 if h == 0 else -1))
            else:
                send(("rb", a, h), asend.at[i, here], afin_in.at[i - 1, here], along_a(a))

        def step_own():
            parts = []
            for h, (o, m) in enumerate(I_ROWS):
                total = line_total(0, h)
                for i, a in enumerate((1, -1)):
                    recv(("rb", a, h), afin_in.at[i, pl.ds(o, m)])
                    total = total + afin_in[i, o:o + m].astype(jnp.float32)
                parts.append(total)
            own = jnp.concatenate(parts, axis=0)
            if c == 0:
                sib_send[...] = own
                send("sib", sib_send.at[pl.ds(SHARD, SHARD)], sib_in, sib)
            else:
                for h in range(2):
                    last_send[h, 0:SHARD] = own[h * SHARD:(h + 1) * SHARD].astype(jnp.bfloat16)
                    last_send[h, SHARD:48] = jnp.zeros((48 - SHARD, D), jnp.bfloat16)
                send(("last", 0), last_send.at[0], last_in, dev(x, y, z - 1, 0))
                send(("last", 1), last_send.at[1], last_in, dev(x, y, z - 1, 1))

        def step_gi():
            if c == 0:
                mine = sib_send[0:SHARD]
            else:
                recv("sib", sib_in)
                mine = sib_in[...]
            recv(("last", c), last_in)
            u, u_inv = unit_rows(pic[...])
            image_dir = mine + last_in[0:SHARD].astype(jnp.float32)
            gi[...] = (image_dir - u * jnp.sum(u * image_dir, axis=1, keepdims=True)) * u_inv

        steps = dict(
            t=step_t, i=step_i, W=step_w, P=step_p, Q=step_q, pp=step_pp, b=step_b, tf=step_tf, gt=step_gt,
            ro=step_ro, rf=step_rf, la=step_la, own=step_own, gi=step_gi,
        )
        for name, *args in ORDER[c]:
            steps[name](*args)
        for cp in started:
            cp.wait_send()

    for c in (0, 1):
        pl.when(core == c)(lambda c=c: one_core(c))


def body(picture_vectors, caption_vectors, scale_exponent, score_shift):
    bf16, f32 = jnp.bfloat16, jnp.float32
    vmem = pl.BlockSpec(memory_space=pltpu.VMEM)
    smem = pl.BlockSpec(memory_space=pltpu.SMEM)
    out = jax.ShapeDtypeStruct((SHARD, D), f32)
    return pl.pallas_call(
        kernel,
        out_shape=(out, out),
        in_specs=[vmem, vmem, smem, smem],
        out_specs=(vmem, vmem),
        scratch_shapes=[
            pltpu.VMEM((SHARD, D), bf16),
            pltpu.VMEM((SHARD, D), bf16),
            pltpu.VMEM((SHARD, D), bf16),
            pltpu.VMEM((N_IMG, D), bf16),
            pltpu.VMEM((N_TXT, D), bf16),
            pltpu.VMEM((N_TXT, N_IMG), bf16),
            pltpu.VMEM((N_TXT, D), f32),
            pltpu.VMEM((N_IMG, D), f32),
            pltpu.VMEM((4, UNIT, D), bf16),
            pltpu.VMEM((4, UNIT, D), bf16),
            pltpu.VMEM((4, UNIT, D), bf16),
            pltpu.VMEM((4, UNIT, D), bf16),
            pltpu.VMEM((UNIT, D), f32),
            pltpu.VMEM((SHARD, D), f32),
            pltpu.VMEM((4, UNIT, D), bf16),
            pltpu.VMEM((8, UNIT, D), bf16),
            pltpu.VMEM((UNIT, D), bf16),
            pltpu.VMEM((2, UNIT, D), bf16),
            pltpu.VMEM((12, UNIT, D), bf16),
            pltpu.VMEM((3, UNIT, D), bf16),
            pltpu.VMEM((2, 48, D), bf16),
            pltpu.VMEM((48, D), bf16),
            pltpu.VMEM((UNIT, D), f32),
            pltpu.VMEM((SHARD, D), f32),
            pltpu.SemaphoreType.DMA((160,)),
            pltpu.SemaphoreType.DMA((160,)),
        ],
        compiler_params=pltpu.CompilerParams(
            collective_id=0, has_side_effects=True, vmem_limit_bytes=56 * 2**20
        ),
    )(picture_vectors, caption_vectors, scale_exponent, score_shift)


def solution(mesh):
    return jax.shard_map(
        body,
        mesh=mesh,
        in_specs=(P(("row", "col"), None), P(("col", "row"), None), P(), P()),
        out_specs=(P(("row", "col"), None), P(("col", "row"), None)),
        check_vma=False,
    )
```

time: 700 us -> 77.2 us (0.11)
  the two profiles are of different devices: /device:TPU:2 before, /device:TPU:1 now
where the time goes in v2:
time: 77.2 us; the launch traced here: 77 us
  Pallas kernels  72.7 us (94%)
  local copies, waits for them, and re-layouts  2.32 us (3%)
  between operations  1.94 us (3%)
    pallas_call x1, Pallas kernels, body(): pl.pallas_call(kernel, out_shape=(out, out), in_specs=[vmem, vmem, smem,...  72.7 us
    unnamed x4, local copies, waits for them, and re-layouts  2.32 us

profile of v2, /device:TPU:1, one launch (start us, length us, event | category | flops | bytes accessed | tf_op | source)
XLA Modules:
  0.0 77.0 jit_solution(14857813508048673760)
XLA Ops:
  1.9 72.7 %shard_map.59 = (f32[40,1152]{1,0:T(8,128)}, f32[40,1152]{1,0:T(8,128)}) custom-call(bf16[40,1152]{1,0:T(8,128)(2,1)} %pic.1, bf16[40,1152]{1,0:T(8,128)(2,1)} %cap.1, f32[1]{0:T(128)S(6)} %copy.8.scale, f32[1]{0:T(128)S(6)} %copy.9.shift), custom_call_target="tpu_custom_call" | custom-call | tf_op jit(solution)/shard_map/pallas_call | solution.py:395
  74.6 0.0 copy-start
  74.6 1.6 %copy.10 = f32[40,1152]{1,0:T(8,128)} copy(f32[40,1152]{1,0:T(8,128)} %get-tuple-element.4) | data formatting | bytes 368640
  76.3 0.0 copy-done
  76.3 0.7 copy.11
Async XLA Ops:
  74.6 1.7 %copy-start = (f32[40,1152]{1,0:T(8,128)S(1)}, f32[40,1152]{1,0:T(8,128)}, u32[]{:S(2)}) copy-start(f32[40,1152]{1,0:T(8,128)} %get-tuple-element.5) | copy-start | bytes 552964

commit v3 on v2

--- a/solution.py
+++ b/solution.py
@@ -20,44 +20,45 @@
 N_TXT = 8 * UNIT
 T_ROWS = ((0, 32), (32, 32), (64, 16))
 I_ROWS = ((0, 48), (48, 32))
+HALF = ((0,), (1,))
 FAR = ((0,), (1, 2))
 T_GROUPS = ((0, 240), (240, 400), (400, 560), (560, 640))
 I_GROUPS = ((0, 640), (640, 1024), (1024, 1280))
 Q_GROUPS = ((896, 1280), (256, 896), (0, 256))
 ORDER = (
     (
-        ('t', 0, 0), ('t', 0, 1), ('t', 0, 2), ('i', 0, 0), ('i', 0, 1), ('i', 1, 0), ('i', 2, 0), ('i', 4, 0),
-        ('i', 5, 0), ('t', 1, 0), ('i', 1, 1), ('i', 2, 1), ('i', 4, 1), ('i', 5, 1), ('t', 1, 1), ('t', 1, 2),
-        ('i', 3, 1), ('t', 2, 0), ('i', 3, 0), ('i', 6, 0), ('i', 7, 0), ('i', 8, 0), ('i', 9, 0), ('t', 2, 1),
-        ('i', 6, 1), ('t', 2, 2), ('i', 12, 0), ('i', 8, 1), ('i', 7, 1), ('W', 0, 0), ('t', 3, 0), ('i', 9, 1),
-        ('W', 1, 0), ('i', 10, 1), ('i', 12, 1), ('t', 3, 1), ('i', 10, 0), ('t', 3, 2), ('i', 11, 1), ('i', 13, 0),
-        ('W', 2, 0), ('i', 11, 0), ('i', 14, 0), ('t', 4, 0), ('W', 0, 1), ('W', 1, 1), ('i', 13, 1), ('W', 2, 1),
-        ('i', 14, 1), ('i', 15, 1), ('W', 3, 0), ('W', 3, 1), ('i', 15, 0), ('W', 0, 2), ('W', 1, 2), ('W', 2, 2),
-        ('W', 3, 2), ('P', 2), ('pp', 3), ('P', 3), ('pp', 0), ('Q', 0), ('ro', 0, 0), ('ro', 0, 1), ('ro', 1, 0),
-        ('ro', 1, 1), ('ro', -1, 0), ('ro', -1, 1), ('ro', 2, 0), ('ro', 2, 1), ('Q', 1), ('rf', 0, -1, 0),
-        ('rf', 0, -1, 1), ('rf', 1, 1, 0), ('rf', 1, 1, 1), ('rf', -1, 1, 0), ('rf', -1, 1, 1), ('rf', 2, -1, 0),
-        ('rf', 2, -1, 1), ('b', 3, 1), ('b', 3, 2), ('b', 0, 0), ('rf', 0, 1, 0), ('rf', 1, -1, 0), ('rf', 0, 1, 1),
-        ('P', 1), ('pp', 2), ('rf', 1, -1, 1), ('rf', 2, 1, 0), ('rf', -1, -1, 0), ('Q', 2), ('rf', 2, 1, 1),
-        ('rf', -1, -1, 1), ('P', 0), ('pp', 1), ('b', 2, 1), ('b', 2, 2), ('b', 3, 0), ('b', 1, 1), ('la', 1, 1),
-        ('b', 1, 2), ('la', 2, 0), ('la', -1, 0), ('la', 2, 1), ('b', 2, 0), ('la', 1, 0), ('la', -1, 1),
-        ('b', 1, 0), ('own',), ('tf',), ('gt',), ('gi',),
+        ('i', 0, 0), ('i', 0, 1), ('t', 0, 0), ('t', 0, 2), ('t', 0, 1), ('i', 4, 0), ('i', 5, 0), ('i', 1, 0),
+        ('i', 2, 0), ('i', 1, 1), ('t', 1, 0), ('i', 2, 1), ('i', 4, 1), ('i', 5, 1), ('t', 1, 2), ('t', 1, 1),
+        ('i', 12, 0), ('i', 3, 1), ('i', 6, 0), ('i', 3, 0), ('t', 2, 0), ('t', 2, 2), ('i', 8, 0), ('i', 7, 0),
+        ('i', 6, 1), ('t', 2, 1), ('i', 8, 1), ('i', 9, 0), ('i', 10, 1), ('i', 7, 1), ('W', 1, 0), ('t', 3, 0),
+        ('W', 0, 0), ('i', 13, 0), ('i', 12, 1), ('i', 9, 1), ('t', 3, 2), ('i', 10, 0), ('i', 11, 1), ('t', 3, 1),
+        ('W', 2, 0), ('i', 14, 0), ('i', 11, 0), ('W', 1, 1), ('i', 13, 1), ('W', 0, 1), ('t', 4, 0), ('i', 14, 1),
+        ('W', 2, 1), ('i', 15, 1), ('W', 3, 0), ('W', 3, 1), ('i', 15, 0), ('W', 0, 2), ('W', 3, 2), ('W', 2, 2),
+        ('W', 1, 2), ('Q', 0), ('ro', -1, 1), ('ro', 1, 1), ('ro', 2, 1), ('ro', 0, 0), ('ro', 2, 0), ('ro', 0, 1),
+        ('ro', 1, 0), ('ro', -1, 0), ('P', 3), ('pp', 0), ('P', 2), ('b', 0, 0), ('pp', 3), ('Q', 1),
+        ('rf', 2, 1, 1), ('rf', -1, -1, 1), ('rf', 1, -1, 1), ('rf', 2, -1, 0), ('rf', 0, -1, 0), ('rf', -1, 1, 0),
+        ('rf', 0, 1, 0), ('rf', 1, 1, 0), ('rf', 2, -1, 1), ('rf', 1, 1, 1), ('rf', 0, -1, 1), ('Q', 2), ('b', 3, 2),
+        ('b', 3, 1), ('rf', 2, 1, 0), ('rf', 1, -1, 0), ('P', 0), ('rf', 0, 1, 1), ('pp', 1), ('b', 3, 0),
+        ('rf', -1, -1, 0), ('P', 1), ('pp', 2), ('rf', -1, 1, 1), ('b', 2, 2), ('b', 2, 1), ('la', 2, 1),
+        ('la', 1, 1), ('b', 2, 0), ('b', 1, 2), ('la', 2, 0), ('b', 1, 1), ('la', -1, 0), ('la', -1, 1), ('b', 1, 0),
+        ('la', 1, 0), ('own',), ('tf',), ('gi',), ('gt',),
     ),
     (
-        ('t', 0, 0), ('t', 0, 1), ('t', 0, 2), ('i', 0, 0), ('i', 0, 1), ('t', 1, 0), ('t', 1, 1), ('t', 1, 2),
-        ('i', 1, 0), ('i', 2, 0), ('i', 4, 0), ('i', 5, 0), ('i', 1, 1), ('i', 2, 1), ('i', 4, 1), ('i', 5, 1),
-        ('t', 2, 0), ('t', 2, 1), ('t', 2, 2), ('i', 6, 0), ('i', 7, 0), ('i', 8, 0), ('i', 9, 0), ('t', 3, 0),
-        ('i', 3, 1), ('i', 6, 1), ('i', 12, 0), ('i', 8, 1), ('i', 7, 1), ('t', 3, 1), ('i', 9, 1), ('i', 13, 0),
-        ('t', 3, 2), ('i', 3, 0), ('W', 0, 0), ('i', 12, 1), ('i', 14, 0), ('W', 1, 0), ('i', 11, 1), ('i', 10, 1),
-        ('W', 2, 0), ('i', 13, 1), ('t', 4, 1), ('i', 14, 1), ('i', 11, 0), ('t', 4, 2), ('W', 3, 0), ('Q', 2),
-        ('i', 10, 0), ('i', 15, 1), ('W', 0, 1), ('W', 1, 1), ('W', 2, 1), ('W', 3, 1), ('Q', 1), ('i', 15, 0),
-        ('rf', 0, -1, 0), ('rf', 0, -1, 1), ('rf', 1, 1, 0), ('rf', 1, 1, 1), ('rf', -1, 1, 0), ('rf', -1, 1, 1),
-        ('W', 0, 2), ('W', 1, 2), ('W', 2, 2), ('W', 3, 2), ('P', 2), ('pp', 3), ('b', 3, 0), ('P', 3), ('pp', 0),
-        ('b', 0, 1), ('b', 0, 2), ('Q', 0), ('ro', 0, 0), ('ro', 0, 1), ('ro', 1, 0), ('ro', 1, 1), ('ro', -1, 0),
-        ('ro', -1, 1), ('ro', 2, 0), ('rf', 2, -1, 0), ('ro', 2, 1), ('rf', 2, -1, 1), ('P', 1), ('pp', 2), ('P', 0),
-        ('pp', 1), ('b', 2, 0), ('rf', 0, 1, 0), ('b', 3, 1), ('rf', 1, -1, 0), ('rf', 0, 1, 1), ('b', 3, 2),
-        ('rf', 1, -1, 1), ('rf', 2, 1, 0), ('rf', -1, -1, 0), ('rf', 2, 1, 1), ('rf', -1, -1, 1), ('b', 1, 0),
-        ('b', 2, 1), ('la', 2, 0), ('b', 2, 2), ('la', 2, 1), ('la', 1, 1), ('la', -1, 0), ('la', 1, 0), ('b', 1, 1),
-        ('la', -1, 1), ('b', 1, 2), ('own',), ('tf',), ('gt',), ('gi',),
+        ('t', 0, 1), ('t', 0, 0), ('t', 0, 2), ('i', 0, 0), ('i', 0, 1), ('t', 1, 1), ('t', 1, 0), ('t', 1, 2),
+        ('i', 4, 0), ('i', 5, 0), ('i', 2, 0), ('i', 1, 0), ('i', 4, 1), ('i', 5, 1), ('t', 2, 1), ('i', 1, 1),
+        ('i', 2, 1), ('t', 2, 0), ('i', 12, 0), ('i', 8, 0), ('t', 2, 2), ('i', 9, 0), ('i', 3, 0), ('i', 6, 0),
+        ('i', 3, 1), ('i', 6, 1), ('i', 7, 0), ('t', 3, 1), ('i', 12, 1), ('i', 8, 1), ('i', 7, 1), ('W', 0, 0),
+        ('t', 3, 0), ('i', 14, 0), ('i', 9, 1), ('t', 3, 2), ('W', 1, 0), ('i', 10, 0), ('i', 11, 0), ('W', 2, 0),
+        ('t', 4, 1), ('i', 13, 0), ('i', 11, 1), ('i', 10, 1), ('W', 2, 1), ('W', 1, 1), ('W', 0, 1), ('t', 4, 2),
+        ('i', 13, 1), ('W', 3, 0), ('i', 14, 1), ('W', 3, 1), ('i', 15, 0), ('Q', 1), ('rf', 0, -1, 0),
+        ('rf', 1, 1, 0), ('rf', 0, -1, 1), ('rf', 1, 1, 1), ('rf', -1, 1, 1), ('i', 15, 1), ('W', 2, 2), ('W', 3, 2),
+        ('rf', -1, 1, 0), ('W', 1, 2), ('W', 0, 2), ('P', 3), ('pp', 0), ('Q', 0), ('ro', 1, 0), ('ro', 1, 1),
+        ('ro', -1, 0), ('ro', 2, 0), ('ro', 2, 1), ('ro', 0, 0), ('ro', -1, 1), ('rf', 2, -1, 1), ('rf', 2, -1, 0),
+        ('ro', 0, 1), ('b', 0, 1), ('b', 0, 2), ('P', 2), ('pp', 3), ('b', 3, 0), ('P', 0), ('pp', 1),
+        ('rf', 1, -1, 0), ('P', 1), ('rf', 1, -1, 1), ('rf', 2, 1, 0), ('pp', 2), ('Q', 2), ('b', 3, 1),
+        ('rf', -1, -1, 0), ('rf', 2, 1, 1), ('b', 3, 2), ('rf', -1, -1, 1), ('rf', 0, 1, 0), ('rf', 0, 1, 1),
+        ('b', 2, 0), ('la', 2, 0), ('la', 2, 1), ('b', 2, 1), ('la', 1, 1), ('b', 2, 2), ('la', -1, 0), ('b', 1, 0),
+        ('la', 1, 0), ('la', -1, 1), ('b', 1, 1), ('b', 1, 2), ('own',), ('tf',), ('gt',), ('gi',),
     ),
 )
 
@@ -187,7 +188,8 @@
 
         def step_t(k, h):
             if k == 0:
-                if h == 0:
+                if "txt" not in got:
+                    got.add("txt")
                     recv("cap", raw_cap)
                     other = unit_rows(raw_cap[...])[0]
                     txt[0:UNIT] = both(own_txt, other) if c == 0 else both(other, own_txt)
@@ -206,7 +208,8 @@
                 send(("i", to_slot, h), img.at[i_piece(s, h)], img.at[i_piece(to_slot, h)], to)
 
             if s == 0:
-                if h == 0:
+                if "img" not in got:
+                    got.add("img")
                     if c == 0:
                         recv("pic_0", raw_a)
                         img[0:UNIT] = both(own_img, unit_rows(raw_a[...])[0])
@@ -219,9 +222,9 @@
             else:
                 need(("i", s, h), img.at[i_piece(s, h)])
             if b == 0:
-                if a == -1 and h == 0:
+                if a == -1 and h in HALF[0]:
                     forward(SLOT[2, 0], along_a(1))
-                if a == 1 and h == 1:
+                if a == 1 and h in HALF[1]:
                     forward(SLOT[2, 0], along_a(-1))
                 forward(SLOT[a, -1], along_b(1))
                 forward(SLOT[a, 1], along_b(-1))
@@ -335,12 +338,12 @@
             here = pl.ds(o, m)
             total = line_total(a, h)
             i = {2: 0, 1: 1, -1: 2}[a]
-            if (a, h) in ((1, 0), (-1, 1)):
+            if (a == 1 and h in HALF[0]) or (a == -1 and h in HALF[1]):
                 recv(("ra", h), half_in.at[here])
                 total = total + half_in[o:o + m].astype(jnp.float32)
             asend[i, o:o + m] = total.astype(jnp.bfloat16)
             if a == 2:
-                send(("ra", h), asend.at[i, here], half_in.at[here], along_a(1 if h == 0 else -1))
+                send(("ra", h), asend.at[i, here], half_in.at[here], along_a(1 if h in HALF[0] else -1))
             else:
                 send(("rb", a, h), asend.at[i, here], afin_in.at[i - 1, here], along_a(a))
 
@@ -426,7 +429,7 @@
             pltpu.SemaphoreType.DMA((160,)),
         ],
         compiler_params=pltpu.CompilerParams(
-            collective_id=0, has_side_effects=True, vmem_limit_bytes=56 * 2**20
+            collective_id=0, has_side_effects=True, vmem_limit_bytes=34 * 2**20
         ),
     )(picture_vectors, caption_vectors, scale_exponent, score_shift)
 

time: 77.2 us -> 74.4 us (0.964)
  Pallas kernels: 72.7 us -> 69.2 us
  local copies, waits for them, and re-layouts: 2.32 us -> 3.12 us
    pallas_call x1, Pallas kernels: 72.7 us -> 69.2 us  [body(): pl.pallas_call(kernel, out_shape=(out, out), in_specs=[vmem, vmem, smem,...]
    unnamed x4 -> x6, local copies, waits for them, and re-layouts: 2.32 us -> 3.12 us
where the time goes in v3:
time: 74.4 us; the launch traced here: 74.2 us
  Pallas kernels  69.2 us (93%)
  local copies, waits for them, and re-layouts  3.12 us (4%)
  between operations  1.94 us (3%)
    pallas_call x1, Pallas kernels, body(): pl.pallas_call(kernel, out_shape=(out, out), in_specs=[vmem, vmem, smem,...  69.2 us
    unnamed x6, local copies, waits for them, and re-layouts  3.12 us

profile of v3, /device:TPU:1, one launch (start us, length us, event | category | flops | bytes accessed | tf_op | source)
XLA Modules:
  0.0 74.2 jit_solution(12743245617525485872)
XLA Ops:
  1.9 0.0 copy-start
  1.9 0.9 %copy-done = bf16[40,1152]{1,0:T(8,128)(2,1)S(1)} copy-done((bf16[40,1152]{1,0:T(8,128)(2,1)S(1)}, bf16[40,1152]{1,0:T(8,128)(2,1)}, u32[]{:S(2)}) %copy-start) | copy-done | bytes 92184
  2.8 0.0 copy-start.1
  2.8 0.9 %copy-done.1 = bf16[40,1152]{1,0:T(8,128)(2,1)S(1)} copy-done((bf16[40,1152]{1,0:T(8,128)(2,1)S(1)}, bf16[40,1152]{1,0:T(8,128)(2,1)}, u32[]{:S(2)}) %copy-start.1) | copy-done | bytes 92184
  3.7 69.2 %shard_map.59 = (f32[40,1152]{1,0:T(8,128)S(1)}, f32[40,1152]{1,0:T(8,128)S(1)}) custom-call(bf16[40,1152]{1,0:T(8,128)(2,1)S(1)} %copy-done, bf16[40,1152]{1,0:T(8,128)(2,1)S(1)} %copy-done.1, f32[1]{0:T(128)S(6)} %copy.8.scale, f32[1]{0:T(128)S(6)} %copy.9.shift), custom_call_target="tpu_custom_call" | custom-call | tf_op jit(solution)/shard_map/pallas_call | solution.py:398
  72.9 0.7 copy.10
  73.6 0.7 copy.11
Async XLA Ops:
  1.9 0.9 %copy-start = (bf16[40,1152]{1,0:T(8,128)(2,1)S(1)}, bf16[40,1152]{1,0:T(8,128)(2,1)}, u32[]{:S(2)}) copy-start(bf16[40,1152]{1,0:T(8,128)(2,1)} %pic.1) | copy-start | bytes 276484
  2.8 0.9 %copy-start.1 = (bf16[40,1152]{1,0:T(8,128)(2,1)S(1)}, bf16[40,1152]{1,0:T(8,128)(2,1)}, u32[]{:S(2)}) copy-start(bf16[40,1152]{1,0:T(8,128)(2,1)} %cap.1) | copy-start | bytes 276484

commit v4 on v3

--- a/solution.py
+++ b/solution.py
@@ -18,47 +18,59 @@
 LINE = (0, 1, -1, 2)
 N_IMG = 16 * UNIT
 N_TXT = 8 * UNIT
-T_ROWS = ((0, 32), (32, 32), (64, 16))
-I_ROWS = ((0, 48), (48, 32))
-HALF = ((0,), (1,))
-FAR = ((0,), (1, 2))
+T_ROWS = ((0, 32), (32, 16), (48, 32))
+I_ROWS = ((0, 32), (32, 16), (48, 32))
+HALF = ((0, 1), (2,))
+FAR = ((1,), (0, 2))
+ROUTE = ({}, {})
+DIRECT = ()
 T_GROUPS = ((0, 240), (240, 400), (400, 560), (560, 640))
 I_GROUPS = ((0, 640), (640, 1024), (1024, 1280))
 Q_GROUPS = ((896, 1280), (256, 896), (0, 256))
 ORDER = (
     (
-        ('i', 0, 0), ('i', 0, 1), ('t', 0, 0), ('t', 0, 2), ('t', 0, 1), ('i', 4, 0), ('i', 5, 0), ('i', 1, 0),
-        ('i', 2, 0), ('i', 1, 1), ('t', 1, 0), ('i', 2, 1), ('i', 4, 1), ('i', 5, 1), ('t', 1, 2), ('t', 1, 1),
-        ('i', 12, 0), ('i', 3, 1), ('i', 6, 0), ('i', 3, 0), ('t', 2, 0), ('t', 2, 2), ('i', 8, 0), ('i', 7, 0),
-        ('i', 6, 1), ('t', 2, 1), ('i', 8, 1), ('i', 9, 0), ('i', 10, 1), ('i', 7, 1), ('W', 1, 0), ('t', 3, 0),
-        ('W', 0, 0), ('i', 13, 0), ('i', 12, 1), ('i', 9, 1), ('t', 3, 2), ('i', 10, 0), ('i', 11, 1), ('t', 3, 1),
-        ('W', 2, 0), ('i', 14, 0), ('i', 11, 0), ('W', 1, 1), ('i', 13, 1), ('W', 0, 1), ('t', 4, 0), ('i', 14, 1),
-        ('W', 2, 1), ('i', 15, 1), ('W', 3, 0), ('W', 3, 1), ('i', 15, 0), ('W', 0, 2), ('W', 3, 2), ('W', 2, 2),
-        ('W', 1, 2), ('Q', 0), ('ro', -1, 1), ('ro', 1, 1), ('ro', 2, 1), ('ro', 0, 0), ('ro', 2, 0), ('ro', 0, 1),
-        ('ro', 1, 0), ('ro', -1, 0), ('P', 3), ('pp', 0), ('P', 2), ('b', 0, 0), ('pp', 3), ('Q', 1),
-        ('rf', 2, 1, 1), ('rf', -1, -1, 1), ('rf', 1, -1, 1), ('rf', 2, -1, 0), ('rf', 0, -1, 0), ('rf', -1, 1, 0),
-        ('rf', 0, 1, 0), ('rf', 1, 1, 0), ('rf', 2, -1, 1), ('rf', 1, 1, 1), ('rf', 0, -1, 1), ('Q', 2), ('b', 3, 2),
-        ('b', 3, 1), ('rf', 2, 1, 0), ('rf', 1, -1, 0), ('P', 0), ('rf', 0, 1, 1), ('pp', 1), ('b', 3, 0),
-        ('rf', -1, -1, 0), ('P', 1), ('pp', 2), ('rf', -1, 1, 1), ('b', 2, 2), ('b', 2, 1), ('la', 2, 1),
-        ('la', 1, 1), ('b', 2, 0), ('b', 1, 2), ('la', 2, 0), ('b', 1, 1), ('la', -1, 0), ('la', -1, 1), ('b', 1, 0),
-        ('la', 1, 0), ('own',), ('tf',), ('gi',), ('gt',),
+        ('t', 0, 0), ('t', 0, 1), ('t', 0, 2), ('i', 0, 2), ('i', 0, 0), ('i', 0, 1), ('i', 5, 2), ('i', 4, 2),
+        ('i', 1, 2), ('i', 2, 2), ('i', 2, 0), ('t', 1, 0), ('i', 1, 0), ('i', 5, 1), ('i', 1, 1), ('i', 4, 0),
+        ('i', 5, 0), ('t', 1, 1), ('i', 2, 1), ('i', 4, 1), ('t', 1, 2), ('i', 12, 2), ('i', 6, 2), ('i', 3, 2),
+        ('i', 3, 0), ('i', 7, 2), ('t', 2, 0), ('i', 3, 1), ('i', 8, 2), ('t', 2, 1), ('i', 8, 0), ('i', 9, 2),
+        ('i', 6, 0), ('i', 6, 1), ('t', 2, 2), ('i', 8, 1), ('i', 9, 0), ('i', 7, 0), ('i', 13, 2), ('t', 3, 0),
+        ('i', 12, 1), ('i', 7, 1), ('W', 1, 0), ('t', 3, 1), ('i', 10, 2), ('i', 12, 0), ('W', 0, 0), ('i', 10, 0),
+        ('i', 10, 1), ('i', 9, 1), ('i', 11, 2), ('t', 3, 2), ('i', 14, 2), ('i', 11, 0), ('i', 14, 0), ('i', 11, 1),
+        ('W', 1, 1), ('W', 2, 1), ('i', 13, 0), ('W', 0, 1), ('t', 4, 1), ('i', 13, 1), ('i', 14, 1), ('W', 2, 0),
+        ('i', 15, 2), ('i', 15, 0), ('i', 15, 1), ('W', 1, 2), ('W', 0, 2), ('W', 2, 2), ('W', 3, 1), ('W', 3, 0),
+        ('W', 3, 2), ('P', 3), ('pp', 0), ('P', 2), ('pp', 3), ('Q', 0), ('ro', 2, 1), ('b', 3, 0), ('b', 3, 2),
+        ('ro', -1, 2), ('ro', 2, 0), ('ro', 2, 2), ('ro', -1, 1), ('ro', 1, 0), ('ro', -1, 0), ('ro', 0, 2),
+        ('ro', 0, 0), ('ro', 1, 2), ('ro', 1, 1), ('b', 0, 1), ('ro', 0, 1), ('P', 1), ('pp', 2), ('Q', 1),
+        ('rf', 2, 1, 0), ('rf', 2, -1, 2), ('rf', 0, -1, 1), ('rf', -1, 1, 0), ('rf', 1, 1, 0), ('rf', 1, 1, 1),
+        ('rf', 1, 1, 2), ('rf', 2, -1, 0), ('rf', 0, -1, 0), ('b', 2, 0), ('rf', 2, 1, 2), ('rf', -1, 1, 1),
+        ('rf', 1, -1, 0), ('rf', 2, 1, 1), ('rf', 2, -1, 1), ('rf', -1, 1, 2), ('rf', -1, -1, 1), ('rf', 0, -1, 2),
+        ('rf', 0, 1, 2), ('rf', -1, -1, 2), ('P', 0), ('pp', 1), ('b', 3, 1), ('po',), ('b', 2, 2), ('rf', 1, -1, 2),
+        ('rf', 0, 1, 1), ('rf', -1, -1, 0), ('rf', 1, -1, 1), ('rf', 0, 1, 0), ('Q', 2), ('la', 2, 0), ('b', 1, 0),
+        ('b', 2, 1), ('la', 2, 2), ('b', 1, 2), ('la', -1, 1), ('la', 2, 1), ('la', 1, 0), ('b', 1, 1),
+        ('la', -1, 2), ('la', 1, 2), ('la', -1, 0), ('la', 1, 1), ('gt',), ('own', 2), ('own', 1), ('own', 0),
+        ('gi',),
     ),
     (
-        ('t', 0, 1), ('t', 0, 0), ('t', 0, 2), ('i', 0, 0), ('i', 0, 1), ('t', 1, 1), ('t', 1, 0), ('t', 1, 2),
-        ('i', 4, 0), ('i', 5, 0), ('i', 2, 0), ('i', 1, 0), ('i', 4, 1), ('i', 5, 1), ('t', 2, 1), ('i', 1, 1),
-        ('i', 2, 1), ('t', 2, 0), ('i', 12, 0), ('i', 8, 0), ('t', 2, 2), ('i', 9, 0), ('i', 3, 0), ('i', 6, 0),
-        ('i', 3, 1), ('i', 6, 1), ('i', 7, 0), ('t', 3, 1), ('i', 12, 1), ('i', 8, 1), ('i', 7, 1), ('W', 0, 0),
-        ('t', 3, 0), ('i', 14, 0), ('i', 9, 1), ('t', 3, 2), ('W', 1, 0), ('i', 10, 0), ('i', 11, 0), ('W', 2, 0),
-        ('t', 4, 1), ('i', 13, 0), ('i', 11, 1), ('i', 10, 1), ('W', 2, 1), ('W', 1, 1), ('W', 0, 1), ('t', 4, 2),
-        ('i', 13, 1), ('W', 3, 0), ('i', 14, 1), ('W', 3, 1), ('i', 15, 0), ('Q', 1), ('rf', 0, -1, 0),
-        ('rf', 1, 1, 0), ('rf', 0, -1, 1), ('rf', 1, 1, 1), ('rf', -1, 1, 1), ('i', 15, 1), ('W', 2, 2), ('W', 3, 2),
-        ('rf', -1, 1, 0), ('W', 1, 2), ('W', 0, 2), ('P', 3), ('pp', 0), ('Q', 0), ('ro', 1, 0), ('ro', 1, 1),
-        ('ro', -1, 0), ('ro', 2, 0), ('ro', 2, 1), ('ro', 0, 0), ('ro', -1, 1), ('rf', 2, -1, 1), ('rf', 2, -1, 0),
-        ('ro', 0, 1), ('b', 0, 1), ('b', 0, 2), ('P', 2), ('pp', 3), ('b', 3, 0), ('P', 0), ('pp', 1),
-        ('rf', 1, -1, 0), ('P', 1), ('rf', 1, -1, 1), ('rf', 2, 1, 0), ('pp', 2), ('Q', 2), ('b', 3, 1),
-        ('rf', -1, -1, 0), ('rf', 2, 1, 1), ('b', 3, 2), ('rf', -1, -1, 1), ('rf', 0, 1, 0), ('rf', 0, 1, 1),
-        ('b', 2, 0), ('la', 2, 0), ('la', 2, 1), ('b', 2, 1), ('la', 1, 1), ('b', 2, 2), ('la', -1, 0), ('b', 1, 0),
-        ('la', 1, 0), ('la', -1, 1), ('b', 1, 1), ('b', 1, 2), ('own',), ('tf',), ('gt',), ('gi',),
+        ('t', 0, 0), ('t', 0, 2), ('t', 0, 1), ('i', 0, 0), ('i', 0, 1), ('i', 0, 2), ('t', 1, 0), ('t', 1, 2),
+        ('i', 4, 0), ('i', 1, 0), ('i', 5, 0), ('t', 1, 1), ('i', 5, 1), ('i', 2, 0), ('i', 1, 1), ('i', 4, 1),
+        ('i', 2, 1), ('i', 5, 2), ('i', 4, 2), ('t', 2, 0), ('i', 1, 2), ('i', 2, 2), ('i', 7, 0), ('i', 6, 0),
+        ('t', 2, 2), ('i', 8, 0), ('i', 12, 0), ('i', 3, 0), ('i', 12, 1), ('i', 6, 1), ('t', 2, 1), ('i', 8, 1),
+        ('i', 3, 1), ('i', 9, 0), ('i', 7, 1), ('i', 6, 2), ('i', 9, 1), ('i', 3, 2), ('i', 8, 2), ('t', 3, 0),
+        ('i', 12, 2), ('i', 13, 0), ('i', 7, 2), ('W', 1, 0), ('i', 14, 0), ('t', 3, 2), ('i', 9, 2), ('W', 0, 0),
+        ('i', 11, 0), ('i', 13, 1), ('t', 3, 1), ('i', 10, 0), ('i', 14, 1), ('i', 11, 1), ('i', 10, 1),
+        ('i', 11, 2), ('W', 2, 0), ('t', 4, 0), ('i', 13, 2), ('i', 10, 2), ('W', 2, 1), ('W', 1, 1), ('W', 0, 1),
+        ('i', 15, 0), ('i', 14, 2), ('t', 4, 2), ('W', 3, 0), ('i', 15, 1), ('W', 3, 1), ('i', 15, 2), ('W', 0, 2),
+        ('W', 2, 2), ('W', 3, 2), ('W', 1, 2), ('P', 2), ('pp', 3), ('P', 3), ('pp', 0), ('Q', 0), ('b', 0, 0),
+        ('ro', 2, 0), ('ro', 1, 1), ('ro', 2, 2), ('ro', 2, 1), ('ro', 1, 0), ('ro', -1, 0), ('b', 0, 2),
+        ('ro', -1, 1), ('ro', 0, 2), ('b', 3, 1), ('ro', 1, 2), ('ro', 0, 0), ('ro', 0, 1), ('ro', -1, 2), ('P', 1),
+        ('pp', 2), ('Q', 1), ('rf', -1, 1, 1), ('rf', 2, 1, 0), ('rf', 2, -1, 0), ('rf', 0, -1, 2), ('rf', 2, -1, 2),
+        ('rf', 2, -1, 1), ('rf', 2, 1, 2), ('rf', 1, 1, 2), ('rf', -1, 1, 0), ('rf', 1, -1, 0), ('rf', 2, 1, 1),
+        ('rf', 1, 1, 0), ('rf', 0, -1, 1), ('rf', 1, 1, 1), ('rf', -1, 1, 2), ('rf', -1, -1, 1), ('rf', -1, -1, 0),
+        ('rf', 0, -1, 0), ('b', 3, 0), ('rf', 0, 1, 2), ('rf', 1, -1, 1), ('Q', 2), ('b', 3, 2), ('rf', 0, 1, 0),
+        ('rf', 1, -1, 2), ('P', 0), ('rf', 0, 1, 1), ('pp', 1), ('la', 2, 0), ('rf', -1, -1, 2), ('b', 2, 1),
+        ('po',), ('la', 2, 2), ('b', 2, 0), ('la', 2, 1), ('la', -1, 1), ('b', 2, 2), ('la', 1, 0), ('la', -1, 0),
+        ('b', 1, 1), ('la', 1, 1), ('la', 1, 2), ('b', 1, 0), ('la', -1, 2), ('b', 1, 2), ('own', 0), ('own', 1),
+        ('own', 2), ('gt',), ('gi',),
     ),
 )
 
@@ -70,10 +82,10 @@
 
 
 def kernel(
-    pic, cap, scale, shift, gi, gt,
+    raw, scale, shift, grads,
     raw_cap, raw_a, raw_b, img, txt, wt, pbuf, qbuf,
-    psend, pd, rsb, rr, tf, tfr,
-    rel_in, fin_in, half_in, afin_in, bsend, asend, last_send, last_in, sib_send, sib_in,
+    psend, pd, rsb, rr, own_in, other,
+    rel_in, fin_in, half_in, afin_in, bsend, asend, last_send, last_in, own_buf, sib_in,
     ssem, rsem,
 ):
     r = lax.axis_index("row")
@@ -92,6 +104,7 @@
     for to in (
         dev(x, y, z, 1 - core), dev(x + 1, y, z, core), dev(x - 1, y, z, core), dev(x, y + 1, z, core),
         dev(x, y - 1, z, core), dev(x, y, z + 2, core), dev(x, y, z - 2, core), dev(x, y, z + 1, 1),
+        dev(x, y, z - 2 + 4 * core, 1 - core),
     ):
         greet(to)
 
@@ -100,6 +113,12 @@
         greet(dev(x, y, z - 1, 1))
         greet(dev(x, y, z - 1, 0))
 
+    for c in DIRECT:
+        @pl.when(core == c)
+        def _(c=c):
+            greet(dev(x + 2 * (1 - c), y + 2 * c, z, c))
+
+    pic, cap = raw.at[0], raw.at[1]
     ids = {}
     offset = shift[0]
 
@@ -153,16 +172,16 @@
             zt = (z + step + 16) % 16
             return row_in + (((zt // 8) * 8 + x * 2) * 32 + y * 8 + zt % 8) * SHARD
 
-        own_txt = unit_rows(cap[...])[0]
-        if c == 0:
-            own_img = unit_rows(pic[...])[0]
-        pl.semaphore_wait(barrier, 10 if c else 8)
+        pl.semaphore_wait(barrier, (11 if c else 9) + (1 if c in DIRECT else 0))
         send("cap", cap, raw_cap, sib)
         if c == 0:
             send("pic_a", pic, raw_a, dev(x, y, z + 1, 1))
         else:
             send("pic_0", pic, raw_a, sib)
             send("pic_b", pic, raw_b, dev(x, y, z + 1, 1))
+        own_txt = unit_rows(cap[...])[0]
+        if c == 0:
+            own_img = unit_rows(pic[...])[0]
 
         def both(one, two):
             return jnp.concatenate([one, two], axis=0).astype(jnp.bfloat16)
@@ -222,16 +241,24 @@
             else:
                 need(("i", s, h), img.at[i_piece(s, h)])
             if b == 0:
-                if a == -1 and h in HALF[0]:
+                if a == -1 and h in HALF[0] and c not in DIRECT:
                     forward(SLOT[2, 0], along_a(1))
-                if a == 1 and h in HALF[1]:
+                if a == 1 and h in HALF[1] and c not in DIRECT:
                     forward(SLOT[2, 0], along_a(-1))
                 forward(SLOT[a, -1], along_b(1))
                 forward(SLOT[a, 1], along_b(-1))
-            if b == -1 and a in RIGHT:
-                forward(SLOT[a, 2], along_b(1))
-            if b == 1 and a not in RIGHT:
-                forward(SLOT[a, 2], along_b(-1))
+                if a == 0 and c in DIRECT:
+                    forward(SLOT[2, 0], along_a(2))
+
+            def way(a):
+                return ROUTE[c].get((a, h), (0, 1) if a in RIGHT else (0, -1))
+
+            if abs(b) == 1 and way(a) == (0, -b):
+                forward(SLOT[a, 2], along_b(-b))
+            if (a, b) == (0, 2):
+                for s_a in (-1, 1):
+                    if way(s_a) == (-s_a, 0):
+                        forward(SLOT[s_a, 2], along_a(-s_a))
 
         def text_needs(slot):
             if slot == 0:
@@ -273,6 +300,14 @@
                 if k > 0 or h in FAR[1 - c]:
                     send(("p", k, h), psend.at[k, pl.ds(o, n)], pd.at[k, pl.ds(o, n)], sib)
 
+        def touches(d, o, n):
+            return o < SHARD if d == 0 else o + n > SHARD
+
+        def own_rows(ref, pieces):
+            mine = [(o, n) for o, n in pieces if touches(c, o, n)]
+            lo, hi = mine[0][0], mine[-1][0] + mine[-1][1]
+            return ref[lo:hi].astype(jnp.float32)[c * SHARD - lo:(c + 1) * SHARD - lo]
+
         def step_b(k, h):
             o, n = T_ROWS[h]
             slot = f_slot(k) if k else 7
@@ -283,20 +318,28 @@
                 recv(("b", more, h), rr.at[k, pl.ds(o, n)])
                 total = total + rr[k, o:o + n].astype(jnp.float32)
             rsb[k, o:o + n] = total.astype(jnp.bfloat16)
-            to = 3 if k == 0 else k - 1
-            send(("b", k, h), rsb.at[k, pl.ds(o, n)], rr.at[to, pl.ds(o, n)], behind)
-
-        def step_tf():
-            for h, (o, n) in enumerate(T_ROWS):
-                recv(("b", 1, h), rr.at[0, pl.ds(o, n)])
-            tf[...] = pbuf[0:UNIT] + rr[0].astype(jnp.float32)
-            send("tf", tf.at[pl.ds((1 - c) * SHARD, SHARD)], tfr, sib)
+            if k == 1:
+                for d in (0, 1):
+                    if touches(d, o, n):
+                        there = own_in.at[c, pl.ds(o, n)]
+                        send(("e", c, h, d), rsb.at[k, pl.ds(o, n)], there, dev(x, y, z - 2 * sg, d))
+            else:
+                to = 3 if k == 0 else k - 1
+                send(("b", k, h), rsb.at[k, pl.ds(o, n)], rr.at[to, pl.ds(o, n)], behind)
+
+        def step_po():
+            send("po", pbuf.at[pl.ds((1 - c) * SHARD, SHARD)], other, sib)
 
         def step_gt():
-            recv("tf", tfr)
+            recv("po", other)
+            text_dir = pbuf[c * SHARD:(c + 1) * SHARD] + other[...]
+            for way in (0, 1):
+                for h, (o, n) in enumerate(T_ROWS):
+                    if touches(c, o, n):
+                        recv(("e", way, h, c), own_in.at[way, pl.ds(o, n)])
+                text_dir = text_dir + own_rows(own_in.at[way], T_ROWS)
             v, v_inv = unit_rows(cap[...])
-            text_dir = tf[c * SHARD:(c + 1) * SHARD] + tfr[...]
-            gt[...] = (text_dir - v * jnp.sum(v * text_dir, axis=1, keepdims=True)) * v_inv
+            grads[1] = (text_dir - v * jnp.sum(v * text_dir, axis=1, keepdims=True)) * v_inv
 
         def q_piece(slot, h):
             o, n = I_ROWS[h]
@@ -347,38 +390,42 @@
             else:
                 send(("rb", a, h), asend.at[i, here], afin_in.at[i - 1, here], along_a(a))
 
-        def step_own():
-            parts = []
-            for h, (o, m) in enumerate(I_ROWS):
-                total = line_total(0, h)
-                for i, a in enumerate((1, -1)):
-                    recv(("rb", a, h), afin_in.at[i, pl.ds(o, m)])
-                    total = total + afin_in[i, o:o + m].astype(jnp.float32)
-                parts.append(total)
-            own = jnp.concatenate(parts, axis=0)
+        def step_own(h):
+            o, m = I_ROWS[h]
+            here = pl.ds(o, m)
+            total = line_total(0, h)
+            for i, a in enumerate((1, -1)):
+                recv(("rb", a, h), afin_in.at[i, here])
+                total = total + afin_in[i, o:o + m].astype(jnp.float32)
             if c == 0:
-                sib_send[...] = own
-                send("sib", sib_send.at[pl.ds(SHARD, SHARD)], sib_in, sib)
-            else:
-                for h in range(2):
-                    last_send[h, 0:SHARD] = own[h * SHARD:(h + 1) * SHARD].astype(jnp.bfloat16)
-                    last_send[h, SHARD:48] = jnp.zeros((48 - SHARD, D), jnp.bfloat16)
-                send(("last", 0), last_send.at[0], last_in, dev(x, y, z - 1, 0))
-                send(("last", 1), last_send.at[1], last_in, dev(x, y, z - 1, 1))
+                own_buf[o:o + m] = total
+                if touches(1, o, m):
+                    p = max(o, SHARD)
+                    send(("s", h), own_buf.at[pl.ds(p, o + m - p)], sib_in.at[pl.ds(p - SHARD, o + m - p)], sib)
+            else:
+                last_send[o:o + m] = total.astype(jnp.bfloat16)
+                for d in (0, 1):
+                    if touches(d, o, m):
+                        send(("l", h, d), last_send.at[here], last_in.at[here], dev(x, y, z - 1, d))
 
         def step_gi():
             if c == 0:
-                mine = sib_send[0:SHARD]
-            else:
-                recv("sib", sib_in)
+                mine = own_buf[0:SHARD]
+            else:
+                for h, (o, m) in enumerate(I_ROWS):
+                    if touches(1, o, m):
+                        p = max(o, SHARD)
+                        recv(("s", h), sib_in.at[pl.ds(p - SHARD, o + m - p)])
                 mine = sib_in[...]
-            recv(("last", c), last_in)
+            for h, (o, m) in enumerate(I_ROWS):
+                if touches(c, o, m):
+                    recv(("l", h, c), last_in.at[pl.ds(o, m)])
+            image_dir = mine + own_rows(last_in, I_ROWS)
             u, u_inv = unit_rows(pic[...])
-            image_dir = mine + last_in[0:SHARD].astype(jnp.float32)
-            gi[...] = (image_dir - u * jnp.sum(u * image_dir, axis=1, keepdims=True)) * u_inv
+            grads[0] = (image_dir - u * jnp.sum(u * image_dir, axis=1, keepdims=True)) * u_inv
 
         steps = dict(
-            t=step_t, i=step_i, W=step_w, P=step_p, Q=step_q, pp=step_pp, b=step_b, tf=step_tf, gt=step_gt,
+            t=step_t, i=step_i, W=step_w, P=step_p, Q=step_q, pp=step_pp, b=step_b, po=step_po, gt=step_gt,
             ro=step_ro, rf=step_rf, la=step_la, own=step_own, gi=step_gi,
         )
         for name, *args in ORDER[c]:
@@ -394,12 +441,12 @@
     bf16, f32 = jnp.bfloat16, jnp.float32
     vmem = pl.BlockSpec(memory_space=pltpu.VMEM)
     smem = pl.BlockSpec(memory_space=pltpu.SMEM)
-    out = jax.ShapeDtypeStruct((SHARD, D), f32)
-    return pl.pallas_call(
+    pairs = jnp.stack([picture_vectors, caption_vectors])
+    grads = pl.pallas_call(
         kernel,
-        out_shape=(out, out),
-        in_specs=[vmem, vmem, smem, smem],
-        out_specs=(vmem, vmem),
+        out_shape=jax.ShapeDtypeStruct((2, SHARD, D), f32),
+        in_specs=[vmem, smem, smem],
+        out_specs=vmem,
         scratch_shapes=[
             pltpu.VMEM((SHARD, D), bf16),
             pltpu.VMEM((SHARD, D), bf16),
@@ -413,7 +460,7 @@
             pltpu.VMEM((4, UNIT, D), bf16),
             pltpu.VMEM((4, UNIT, D), bf16),
             pltpu.VMEM((4, UNIT, D), bf16),
-            pltpu.VMEM((UNIT, D), f32),
+            pltpu.VMEM((2, UNIT, D), bf16),
             pltpu.VMEM((SHARD, D), f32),
             pltpu.VMEM((4, UNIT, D), bf16),
             pltpu.VMEM((8, UNIT, D), bf16),
@@ -421,17 +468,18 @@
             pltpu.VMEM((2, UNIT, D), bf16),
             pltpu.VMEM((12, UNIT, D), bf16),
             pltpu.VMEM((3, UNIT, D), bf16),
-            pltpu.VMEM((2, 48, D), bf16),
-            pltpu.VMEM((48, D), bf16),
+            pltpu.VMEM((UNIT, D), bf16),
+            pltpu.VMEM((UNIT, D), bf16),
             pltpu.VMEM((UNIT, D), f32),
             pltpu.VMEM((SHARD, D), f32),
-            pltpu.SemaphoreType.DMA((160,)),
-            pltpu.SemaphoreType.DMA((160,)),
+            pltpu.SemaphoreType.DMA((192,)),
+            pltpu.SemaphoreType.DMA((192,)),
         ],
         compiler_params=pltpu.CompilerParams(
             collective_id=0, has_side_effects=True, vmem_limit_bytes=34 * 2**20
         ),
-    )(picture_vectors, caption_vectors, scale_exponent, score_shift)
+    )(pairs, scale_exponent, score_shift)
+    return grads[0], grads[1]
 
 
 def solution(mesh):

time: 74.4 us -> 71.9 us (0.966)
  local copies, waits for them, and re-layouts: 3.12 us -> 0.76 us
  Pallas kernels: 69.2 us -> 68 us
  other arithmetic: 0 us -> 0.96 us
    unnamed x6 -> x0, local copies, waits for them, and re-layouts: 3.12 us -> none
    pallas_call x1, Pallas kernels: 69.2 us -> 68 us  [body(): pl.pallas_call(kernel, out_shape=jax.ShapeDtypeStruct((2, SHARD, D), f32)...]
    another operation x0 -> x1, other arithmetic: none -> 0.96 us  [body(): pairs = jnp.stack([picture_vectors, caption_vectors])]
    squeeze x0 -> x1, local copies, waits for them, and re-layouts: none -> 0.76 us  [body(): return (grads[0], grads[1])]
where the time goes in v4:
time: 71.9 us; the launch traced here: 71.7 us
  Pallas kernels  68 us (95%)
  between operations  1.93 us (3%)
  other arithmetic  0.96 us (1%)
  local copies, waits for them, and re-layouts  0.76 us (1%)
    pallas_call x1, Pallas kernels, body(): pl.pallas_call(kernel, out_shape=jax.ShapeDtypeStruct((2, SHARD, D), f32)...  68 us

profile of v4, /device:TPU:1, one launch (start us, length us, event | category | flops | bytes accessed | tf_op | source)
XLA Modules:
  0.0 71.7 jit_solution(8809460023497247793)
XLA Ops:
  1.9 1.0 %pad_maximum_fusion.raw = bf16[2,40,1152]{2,1,0:T(8,128)(2,1)S(1)} fusion(bf16[1,40,1152]{2,1,0:T(8,128)(2,1)} %bitcast.6, bf16[1,40,1152]{2,1,0:T(8,128)(2,1)} %bitcast.7), kind=kLoop, calls=%fused_computation | loop fusion | flops 92160 | bytes 368640 | tf_op jit(solution)/shard_map/stack | solution.py:444
  2.9 68.0 %shard_map.59 = f32[2,40,1152]{2,1,0:T(8,128)S(1)} custom-call(bf16[2,40,1152]{2,1,0:T(8,128)(2,1)S(1)} %pad_maximum_fusion.raw, f32[1]{0:T(128)S(6)} %copy.6.scale, f32[1]{0:T(128)S(6)} %copy.7.shift), custom_call_target="tpu_custom_call" | custom-call | tf_op jit(solution)/shard_map/pallas_call | solution.py:445
  70.9 0.8 %slice_bitcast_fusion = (f32[40,1152]{1,0:T(8,128)}, f32[40,1152]{1,0:T(8,128)}) fusion(f32[2,40,1152]{2,1,0:T(8,128)S(1)} %shard_map.59), kind=kLoop, calls=%fused_computation.1 | loop fusion | bytes 737280 | tf_op jit(solution)/shard_map/squeeze | solution.py:482

commit v5 on v4

--- a/solution.py
+++ b/solution.py
@@ -24,53 +24,51 @@
 FAR = ((1,), (0, 2))
 ROUTE = ({}, {})
 DIRECT = ()
-T_GROUPS = ((0, 240), (240, 400), (400, 560), (560, 640))
-I_GROUPS = ((0, 640), (640, 1024), (1024, 1280))
+W_BLOCKS = ((0, 240, 0, 640), (240, 400, 0, 640), (0, 400, 640, 1024), (400, 640, 0, 1024), (0, 640, 1024, 1280))
+P_GROUPS = ((400, 640, 0, 1280), (240, 400, 0, 1280), (0, 240, 0, 1280))
 Q_GROUPS = ((896, 1280), (256, 896), (0, 256))
 ORDER = (
     (
-        ('t', 0, 0), ('t', 0, 1), ('t', 0, 2), ('i', 0, 2), ('i', 0, 0), ('i', 0, 1), ('i', 5, 2), ('i', 4, 2),
-        ('i', 1, 2), ('i', 2, 2), ('i', 2, 0), ('t', 1, 0), ('i', 1, 0), ('i', 5, 1), ('i', 1, 1), ('i', 4, 0),
-        ('i', 5, 0), ('t', 1, 1), ('i', 2, 1), ('i', 4, 1), ('t', 1, 2), ('i', 12, 2), ('i', 6, 2), ('i', 3, 2),
-        ('i', 3, 0), ('i', 7, 2), ('t', 2, 0), ('i', 3, 1), ('i', 8, 2), ('t', 2, 1), ('i', 8, 0), ('i', 9, 2),
-        ('i', 6, 0), ('i', 6, 1), ('t', 2, 2), ('i', 8, 1), ('i', 9, 0), ('i', 7, 0), ('i', 13, 2), ('t', 3, 0),
-        ('i', 12, 1), ('i', 7, 1), ('W', 1, 0), ('t', 3, 1), ('i', 10, 2), ('i', 12, 0), ('W', 0, 0), ('i', 10, 0),
-        ('i', 10, 1), ('i', 9, 1), ('i', 11, 2), ('t', 3, 2), ('i', 14, 2), ('i', 11, 0), ('i', 14, 0), ('i', 11, 1),
-        ('W', 1, 1), ('W', 2, 1), ('i', 13, 0), ('W', 0, 1), ('t', 4, 1), ('i', 13, 1), ('i', 14, 1), ('W', 2, 0),
-        ('i', 15, 2), ('i', 15, 0), ('i', 15, 1), ('W', 1, 2), ('W', 0, 2), ('W', 2, 2), ('W', 3, 1), ('W', 3, 0),
-        ('W', 3, 2), ('P', 3), ('pp', 0), ('P', 2), ('pp', 3), ('Q', 0), ('ro', 2, 1), ('b', 3, 0), ('b', 3, 2),
-        ('ro', -1, 2), ('ro', 2, 0), ('ro', 2, 2), ('ro', -1, 1), ('ro', 1, 0), ('ro', -1, 0), ('ro', 0, 2),
-        ('ro', 0, 0), ('ro', 1, 2), ('ro', 1, 1), ('b', 0, 1), ('ro', 0, 1), ('P', 1), ('pp', 2), ('Q', 1),
-        ('rf', 2, 1, 0), ('rf', 2, -1, 2), ('rf', 0, -1, 1), ('rf', -1, 1, 0), ('rf', 1, 1, 0), ('rf', 1, 1, 1),
-        ('rf', 1, 1, 2), ('rf', 2, -1, 0), ('rf', 0, -1, 0), ('b', 2, 0), ('rf', 2, 1, 2), ('rf', -1, 1, 1),
-        ('rf', 1, -1, 0), ('rf', 2, 1, 1), ('rf', 2, -1, 1), ('rf', -1, 1, 2), ('rf', -1, -1, 1), ('rf', 0, -1, 2),
-        ('rf', 0, 1, 2), ('rf', -1, -1, 2), ('P', 0), ('pp', 1), ('b', 3, 1), ('po',), ('b', 2, 2), ('rf', 1, -1, 2),
-        ('rf', 0, 1, 1), ('rf', -1, -1, 0), ('rf', 1, -1, 1), ('rf', 0, 1, 0), ('Q', 2), ('la', 2, 0), ('b', 1, 0),
-        ('b', 2, 1), ('la', 2, 2), ('b', 1, 2), ('la', -1, 1), ('la', 2, 1), ('la', 1, 0), ('b', 1, 1),
-        ('la', -1, 2), ('la', 1, 2), ('la', -1, 0), ('la', 1, 1), ('gt',), ('own', 2), ('own', 1), ('own', 0),
-        ('gi',),
+        ('t', 0, 1), ('i', 0, 0), ('i', 0, 1), ('i', 0, 2), ('t', 0, 0), ('t', 0, 2), ('i', 4, 0), ('i', 5, 0),
+        ('i', 2, 0), ('i', 1, 0), ('i', 2, 1), ('t', 1, 1), ('i', 5, 1), ('i', 1, 1), ('i', 4, 1), ('i', 1, 2),
+        ('i', 2, 2), ('i', 4, 2), ('i', 5, 2), ('t', 1, 0), ('t', 1, 2), ('i', 12, 0), ('i', 8, 0), ('i', 3, 0),
+        ('t', 2, 1), ('i', 3, 1), ('i', 3, 2), ('i', 9, 0), ('i', 6, 0), ('i', 8, 1), ('i', 6, 1), ('t', 2, 0),
+        ('i', 7, 0), ('i', 6, 2), ('i', 9, 1), ('i', 8, 2), ('t', 2, 2), ('i', 12, 1), ('i', 7, 1), ('t', 3, 1),
+        ('i', 7, 2), ('i', 14, 0), ('W', 0), ('i', 9, 2), ('i', 10, 0), ('W', 1), ('t', 3, 0), ('i', 10, 1),
+        ('i', 12, 2), ('i', 10, 2), ('i', 11, 0), ('i', 11, 1), ('i', 13, 0), ('i', 14, 1), ('t', 3, 2),
+        ('i', 13, 1), ('i', 11, 2), ('W', 2), ('t', 4, 1), ('i', 13, 2), ('i', 14, 2), ('i', 15, 0), ('i', 15, 1),
+        ('i', 15, 2), ('W', 4), ('W', 3), ('P', 0), ('pp', 0), ('pp', 3), ('b', 0, 1), ('b', 3, 0), ('b', 3, 2),
+        ('Q', 0), ('ro', -1, 2), ('ro', 2, 1), ('ro', 2, 0), ('ro', -1, 1), ('ro', -1, 0), ('ro', 2, 2),
+        ('ro', 1, 2), ('ro', 1, 0), ('ro', 0, 2), ('ro', 0, 1), ('ro', 1, 1), ('ro', 0, 0), ('P', 1), ('pp', 2),
+        ('Q', 1), ('rf', 2, -1, 1), ('rf', 2, -1, 2), ('rf', 1, 1, 1), ('rf', 2, -1, 0), ('b', 3, 1),
+        ('rf', 1, 1, 2), ('b', 2, 0), ('rf', 2, 1, 1), ('rf', 2, 1, 0), ('rf', -1, -1, 0), ('rf', 2, 1, 2),
+        ('rf', -1, -1, 2), ('rf', 0, -1, 2), ('rf', -1, 1, 2), ('rf', -1, 1, 0), ('rf', 0, -1, 0), ('rf', 1, 1, 0),
+        ('rf', 1, -1, 2), ('rf', 0, 1, 2), ('rf', -1, 1, 1), ('rf', -1, -1, 1), ('rf', 0, -1, 1), ('Q', 2),
+        ('rf', 1, -1, 1), ('b', 2, 2), ('rf', 1, -1, 0), ('rf', 0, 1, 1), ('rf', 0, 1, 0), ('P', 2), ('pp', 1),
+        ('po',), ('la', 2, 1), ('b', 2, 1), ('la', 2, 0), ('b', 1, 0), ('la', 2, 2), ('b', 1, 2), ('b', 1, 1),
+        ('la', -1, 0), ('la', -1, 2), ('la', 1, 2), ('la', -1, 1), ('la', 1, 1), ('la', 1, 0), ('own', 2), ('gt',),
+        ('own', 1), ('own', 0), ('gi',),
     ),
     (
         ('t', 0, 0), ('t', 0, 2), ('t', 0, 1), ('i', 0, 0), ('i', 0, 1), ('i', 0, 2), ('t', 1, 0), ('t', 1, 2),
-        ('i', 4, 0), ('i', 1, 0), ('i', 5, 0), ('t', 1, 1), ('i', 5, 1), ('i', 2, 0), ('i', 1, 1), ('i', 4, 1),
-        ('i', 2, 1), ('i', 5, 2), ('i', 4, 2), ('t', 2, 0), ('i', 1, 2), ('i', 2, 2), ('i', 7, 0), ('i', 6, 0),
-        ('t', 2, 2), ('i', 8, 0), ('i', 12, 0), ('i', 3, 0), ('i', 12, 1), ('i', 6, 1), ('t', 2, 1), ('i', 8, 1),
-        ('i', 3, 1), ('i', 9, 0), ('i', 7, 1), ('i', 6, 2), ('i', 9, 1), ('i', 3, 2), ('i', 8, 2), ('t', 3, 0),
-        ('i', 12, 2), ('i', 13, 0), ('i', 7, 2), ('W', 1, 0), ('i', 14, 0), ('t', 3, 2), ('i', 9, 2), ('W', 0, 0),
-        ('i', 11, 0), ('i', 13, 1), ('t', 3, 1), ('i', 10, 0), ('i', 14, 1), ('i', 11, 1), ('i', 10, 1),
-        ('i', 11, 2), ('W', 2, 0), ('t', 4, 0), ('i', 13, 2), ('i', 10, 2), ('W', 2, 1), ('W', 1, 1), ('W', 0, 1),
-        ('i', 15, 0), ('i', 14, 2), ('t', 4, 2), ('W', 3, 0), ('i', 15, 1), ('W', 3, 1), ('i', 15, 2), ('W', 0, 2),
-        ('W', 2, 2), ('W', 3, 2), ('W', 1, 2), ('P', 2), ('pp', 3), ('P', 3), ('pp', 0), ('Q', 0), ('b', 0, 0),
-        ('ro', 2, 0), ('ro', 1, 1), ('ro', 2, 2), ('ro', 2, 1), ('ro', 1, 0), ('ro', -1, 0), ('b', 0, 2),
-        ('ro', -1, 1), ('ro', 0, 2), ('b', 3, 1), ('ro', 1, 2), ('ro', 0, 0), ('ro', 0, 1), ('ro', -1, 2), ('P', 1),
-        ('pp', 2), ('Q', 1), ('rf', -1, 1, 1), ('rf', 2, 1, 0), ('rf', 2, -1, 0), ('rf', 0, -1, 2), ('rf', 2, -1, 2),
-        ('rf', 2, -1, 1), ('rf', 2, 1, 2), ('rf', 1, 1, 2), ('rf', -1, 1, 0), ('rf', 1, -1, 0), ('rf', 2, 1, 1),
-        ('rf', 1, 1, 0), ('rf', 0, -1, 1), ('rf', 1, 1, 1), ('rf', -1, 1, 2), ('rf', -1, -1, 1), ('rf', -1, -1, 0),
-        ('rf', 0, -1, 0), ('b', 3, 0), ('rf', 0, 1, 2), ('rf', 1, -1, 1), ('Q', 2), ('b', 3, 2), ('rf', 0, 1, 0),
-        ('rf', 1, -1, 2), ('P', 0), ('rf', 0, 1, 1), ('pp', 1), ('la', 2, 0), ('rf', -1, -1, 2), ('b', 2, 1),
-        ('po',), ('la', 2, 2), ('b', 2, 0), ('la', 2, 1), ('la', -1, 1), ('b', 2, 2), ('la', 1, 0), ('la', -1, 0),
-        ('b', 1, 1), ('la', 1, 1), ('la', 1, 2), ('b', 1, 0), ('la', -1, 2), ('b', 1, 2), ('own', 0), ('own', 1),
-        ('own', 2), ('gt',), ('gi',),
+        ('i', 1, 0), ('i', 4, 0), ('i', 5, 0), ('i', 2, 0), ('t', 1, 1), ('i', 4, 1), ('i', 1, 1), ('i', 5, 1),
+        ('i', 2, 1), ('i', 4, 2), ('i', 1, 2), ('i', 5, 2), ('i', 2, 2), ('t', 2, 0), ('i', 7, 0), ('i', 6, 0),
+        ('i', 12, 0), ('i', 8, 0), ('i', 3, 0), ('t', 2, 2), ('i', 6, 1), ('i', 8, 1), ('i', 9, 0), ('i', 3, 1),
+        ('t', 2, 1), ('i', 7, 1), ('i', 12, 1), ('i', 6, 2), ('i', 9, 1), ('i', 3, 2), ('i', 8, 2), ('i', 7, 2),
+        ('W', 1), ('t', 3, 0), ('i', 13, 0), ('i', 12, 2), ('W', 0), ('i', 14, 0), ('i', 9, 2), ('i', 10, 0),
+        ('t', 3, 2), ('i', 11, 0), ('i', 13, 1), ('i', 11, 1), ('i', 14, 1), ('t', 3, 1), ('i', 10, 1), ('i', 11, 2),
+        ('i', 13, 2), ('i', 10, 2), ('W', 2), ('t', 4, 0), ('i', 14, 2), ('i', 15, 0), ('i', 15, 1), ('i', 15, 2),
+        ('t', 4, 2), ('W', 3), ('W', 4), ('P', 0), ('pp', 3), ('pp', 0), ('Q', 0), ('ro', -1, 0), ('ro', 2, 0),
+        ('ro', 2, 2), ('ro', 1, 0), ('ro', -1, 1), ('ro', 1, 2), ('ro', -1, 2), ('ro', 1, 1), ('ro', 2, 1),
+        ('ro', 0, 2), ('ro', 0, 0), ('b', 0, 0), ('ro', 0, 1), ('b', 0, 2), ('P', 1), ('b', 3, 1), ('pp', 2),
+        ('Q', 1), ('rf', 2, -1, 1), ('rf', 2, 1, 0), ('rf', 2, -1, 0), ('rf', -1, 1, 2), ('rf', 1, 1, 1),
+        ('rf', 2, 1, 2), ('rf', -1, -1, 1), ('rf', 2, 1, 1), ('rf', 2, -1, 2), ('rf', -1, 1, 1), ('rf', -1, -1, 0),
+        ('rf', 1, 1, 2), ('rf', 0, -1, 1), ('rf', 1, -1, 0), ('rf', -1, 1, 0), ('rf', 1, 1, 0), ('rf', 0, -1, 2),
+        ('rf', 0, -1, 0), ('rf', 1, -1, 2), ('b', 3, 0), ('rf', 0, 1, 2), ('P', 2), ('pp', 1), ('b', 3, 2),
+        ('rf', -1, -1, 2), ('rf', 1, -1, 1), ('rf', 0, 1, 1), ('po',), ('rf', 0, 1, 0), ('Q', 2), ('la', 2, 0),
+        ('b', 2, 1), ('la', 2, 2), ('la', 2, 1), ('la', -1, 1), ('b', 2, 0), ('la', -1, 0), ('b', 2, 2),
+        ('la', 1, 0), ('b', 1, 1), ('la', 1, 2), ('la', -1, 2), ('la', 1, 1), ('b', 1, 0), ('own', 0), ('b', 1, 2),
+        ('own', 2), ('own', 1), ('gt',), ('gi',),
     ),
 )
 
@@ -269,9 +267,8 @@
                 if not mine:
                     need(("g", k, h), txt.at[t_piece(slot, h)])
 
-        def step_w(gt_, gi_):
-            t0, t1 = T_GROUPS[gt_]
-            i0, i1 = I_GROUPS[gi_]
+        def step_w(n):
+            t0, t1, i0, i1 = W_BLOCKS[n]
             for s in range(t0 // UNIT, t1 // UNIT):
                 text_needs(s)
             dots = lax.dot_general(
@@ -284,8 +281,9 @@
             wt[t0:t1, i0:i1] = jnp.where(match, -value, value).astype(jnp.bfloat16)
 
         def step_p(g):
-            t0, t1 = T_GROUPS[g]
-            pbuf[t0:t1] = jnp.dot(wt[t0:t1], img[...], preferred_element_type=jnp.float32)
+            t0, t1, k0, k1 = P_GROUPS[g]
+            part = jnp.dot(wt[t0:t1, k0:k1], img[k0:k1], preferred_element_type=jnp.float32)
+            pbuf[t0:t1] = part if k0 == 0 else pbuf[t0:t1] + part
 
         def step_q(g):
             i0, i1 = Q_GROUPS[g]

time: 71.9 us -> 69.5 us (0.967)
  Pallas kernels: 68 us -> 65.7 us
    pallas_call x1, Pallas kernels: 68 us -> 65.7 us  [body(): pl.pallas_call(kernel, out_shape=jax.ShapeDtypeStruct((2, SHARD, D), f32)...]
where the time goes in v5:
time: 69.5 us; the launch traced here: 69.4 us
  Pallas kernels  65.7 us (95%)
  between operations  1.93 us (3%)
  other arithmetic  0.96 us (1%)
  local copies, waits for them, and re-layouts  0.76 us (1%)
    pallas_call x1, Pallas kernels, body(): pl.pallas_call(kernel, out_shape=jax.ShapeDtypeStruct((2, SHARD, D), f32)...  65.7 us

profile of v5, /device:TPU:1, one launch (start us, length us, event | category | flops | bytes accessed | tf_op | source)
XLA Modules:
  0.0 69.4 jit_solution(12094306728096741510)
XLA Ops:
  1.9 1.0 %pad_maximum_fusion.raw = bf16[2,40,1152]{2,1,0:T(8,128)(2,1)S(1)} fusion(bf16[1,40,1152]{2,1,0:T(8,128)(2,1)} %bitcast.6, bf16[1,40,1152]{2,1,0:T(8,128)(2,1)} %bitcast.7), kind=kLoop, calls=%fused_computation | loop fusion | flops 92160 | bytes 368640 | tf_op jit(solution)/shard_map/stack | solution.py:442
  2.9 65.7 %shard_map.59 = f32[2,40,1152]{2,1,0:T(8,128)S(1)} custom-call(bf16[2,40,1152]{2,1,0:T(8,128)(2,1)S(1)} %pad_maximum_fusion.raw, f32[1]{0:T(128)S(6)} %copy.6.scale, f32[1]{0:T(128)S(6)} %copy.7.shift), custom_call_target="tpu_custom_call" | custom-call | tf_op jit(solution)/shard_map/pallas_call | solution.py:443
  68.6 0.8 %slice_bitcast_fusion = (f32[40,1152]{1,0:T(8,128)}, f32[40,1152]{1,0:T(8,128)}) fusion(f32[2,40,1152]{2,1,0:T(8,128)S(1)} %shard_map.59), kind=kLoop, calls=%fused_computation.1 | loop fusion | bytes 737280 | tf_op jit(solution)/shard_map/squeeze | solution.py:480
